TPU v7x, 32 devices: a whole 2x2x4 slice. The times are simulated.
32 devices in a mesh: lon: 4 (over z), lat: 4 (over y, core), batch: 2 (over x).
Axes of the slice: x: 2, y: 2, z: 4, core: 2. Of those that a mesh axis runs over, the one named last changes fastest.
Arguments:
- attn_input: bfloat16 [16, 24, 48, 192], P('batch', 'lat', 'lon'), parts along dimension 0, may hold values from -6 to 6
- out_grad: bfloat16 [16, 24, 48, 192], P('batch', 'lat', 'lon'), parts along dimension 0, may hold values from -6 to 6
- w_qkv: bfloat16 [192, 576], replicated, may hold values from -0.4375 to 0.4375
- w_proj: bfloat16 [192, 192], replicated, may hold values from -0.4375 to 0.4375
- bias_table: float32 [4, 4, 6, 2, 2, 6, 6, 23], P(None, 'lat'), may hold values from -1 to 401
- mask_ids: int32 [16, 24, 48], P('batch', 'lat', 'lon'), parts along dimension 0, may hold values from 0 to 2
- valid_rows: int32 [2], P('batch'), parts along dimension 0, may hold values from 12 to 24
Outputs:
- grad_input: bfloat16 [16, 24, 48, 192], P('batch', 'lat', 'lon'), parts along dimension 0
- grad_qkv: float32 [384, 576], P('batch'), parts along dimension 0
- grad_proj: float32 [384, 192], P('batch'), parts along dimension 0
- grad_bias: float32 [8, 4, 6, 2, 2, 6, 6, 23], P('batch', 'lat'), parts along dimension 0
There are 2 independent parts, one for each index of `batch`. A program takes and returns all parts, laid end to end along the dimension named above; an argument that names none is the same for every part. Nothing has to cross between parts.
All inputs are finite; a program needn't handle non-finite values.
Results may differ from a plain program's by a relative error of at most 0.0075.
Values may be sent and summed in bfloat16 or wider, within the bound.
A program may use at most 192 MiB of HBM per device.

v0:
```python
import jax
import jax.numpy as jnp
from jax import lax
from jax.sharding import PartitionSpec as P

C = 192
HEADS = 6
HEAD_DIM = 32
WZ = 2
WLAT = 6
WLON = 12
WIN = 144


masked_score = -1000000000.0


def from_behind(shard, axis, by):
    devices = lax.axis_size(axis)
    return lax.ppermute(shard, axis, [(i, (i + by) % devices) for i in range(devices)])


def shifted_2(shard, axis, by):
    devices = lax.axis_size(axis)
    pairs = [(i, i + by) for i in range(devices) if 0 <= i + by < devices]
    return lax.ppermute(shard, axis, pairs)


def lon_table():
    column = jnp.arange(WLON, dtype=jnp.int32)
    offset = jnp.arange(2 * WLON - 1, dtype=jnp.int32)
    return (
        column[:, None, None] - column[None, :, None] + (WLON - 1) == offset[None, None, :]
    ).astype(jnp.float32)


def expand_bias(folded):
    expanded = jnp.einsum(
        "...hxyuvr,abr->...hxuayvb", folded, lon_table(), precision=lax.Precision.HIGHEST
    )
    return expanded.reshape(expanded.shape[:-7] + (HEADS, WIN, WIN))


def fold_bias(grads):
    divided = grads.reshape(grads.shape[:-3] + (HEADS, WZ, WLAT, WLON, WZ, WLAT, WLON))
    return jnp.einsum(
        "...hxuayvb,abr->...hxyuvr", divided, lon_table(), precision=lax.Precision.HIGHEST
    )


def to_windows(grid_field):
    levels, lat_rows, lon_cols = grid_field.shape[:3]
    trailing = grid_field.shape[3:]
    divided = grid_field.reshape(
        (levels // WZ, WZ, lat_rows // WLAT, WLAT, lon_cols // WLON, WLON) + trailing
    )
    arrangement = (0, 2, 4, 1, 3, 5) + tuple(range(6, 6 + len(trailing)))
    return divided.transpose(arrangement).reshape(
        (levels // WZ, lat_rows // WLAT, lon_cols // WLON, WIN) + trailing
    )


def from_windows(windows, levels, lat_rows, lon_cols):
    trailing = windows.shape[4:]
    divided = windows.reshape(
        (levels // WZ, lat_rows // WLAT, lon_cols // WLON, WZ, WLAT, WLON) + trailing
    )
    arrangement = (0, 3, 1, 4, 2, 5) + tuple(range(6, 6 + len(trailing)))
    return divided.transpose(arrangement).reshape((levels, lat_rows, lon_cols) + trailing)


def outer_part(grid_field, cut_width, axis, leading):
    length = grid_field.shape[axis]
    if leading:
        return lax.slice_in_dim(grid_field, 0, cut_width, axis=axis)
    return lax.slice_in_dim(grid_field, length - cut_width, length, axis=axis)


def inner_part(grid_field, cut_width, axis, leading):
    length = grid_field.shape[axis]
    if leading:
        return lax.slice_in_dim(grid_field, cut_width, length, axis=axis)
    return lax.slice_in_dim(grid_field, 0, length - cut_width, axis=axis)


def attach(kept, arrived, axis, leading):
    if leading:
        return jnp.concatenate([kept, arrived], axis=axis)
    return jnp.concatenate([arrived, kept], axis=axis)


def displace(fields, heading):
    leading = heading < 0
    fields = [jnp.roll(grid_field, heading * (WZ // 2), axis=0) for grid_field in fields]
    border = jnp.stack([outer_part(grid_field, WLON // 2, 2, leading) for grid_field in fields])
    arrived = from_behind(border, "lon", heading)
    fields = [
        attach(inner_part(grid_field, WLON // 2, 2, leading), arrived[number], 2, leading)
        for number, grid_field in enumerate(fields)
    ]
    border = jnp.stack([outer_part(grid_field, WLAT // 2, 1, leading) for grid_field in fields])
    arrived = shifted_2(border, "lat", heading)
    return [
        attach(inner_part(grid_field, WLAT // 2, 1, leading), arrived[number], 1, leading)
        for number, grid_field in enumerate(fields)
    ]


def window_backward(shifted, grads_y, allowed, bias, w_qkv, w_proj):
    groups = shifted.shape[0]
    flattened = shifted.reshape(groups * WIN, C)
    projected = jnp.dot(flattened, w_qkv, preferred_element_type=jnp.float32).astype(jnp.bfloat16)
    projected = projected.reshape(groups, WIN, 3, HEADS, HEAD_DIM)
    query_rows = projected[:, :, 0]
    key_rows = projected[:, :, 1]
    value_rows = projected[:, :, 2]
    temper = HEAD_DIM ** (-0.5)
    scores = (
        jnp.einsum("gnhd,gmhd->ghnm", query_rows, key_rows, preferred_element_type=jnp.float32)
        * temper
        + bias
    )
    scores = jnp.where(allowed[:, None], scores, masked_score)
    exponent = jnp.exp(scores - jnp.max(scores, axis=-1, keepdims=True))
    attn_probs = exponent / jnp.sum(exponent, axis=-1, keepdims=True)
    probs_low = attn_probs.astype(jnp.bfloat16)
    attended = jnp.einsum(
        "ghnm,gmhd->gnhd", probs_low, value_rows, preferred_element_type=jnp.float32
    )
    attended = attended.astype(jnp.bfloat16).reshape(groups * WIN, C)
    upstream = grads_y.reshape(groups * WIN, C)
    grad_proj = jnp.einsum("tc,te->ce", attended, upstream, preferred_element_type=jnp.float32)
    grad_att = jnp.einsum("te,ce->tc", upstream, w_proj, preferred_element_type=jnp.float32)
    grad_att = grad_att.astype(jnp.bfloat16).reshape(groups, WIN, HEADS, HEAD_DIM)
    grad_prob = jnp.einsum(
        "gnhd,gmhd->ghnm", grad_att, value_rows, preferred_element_type=jnp.float32
    )
    grad_score = attn_probs * (grad_prob - jnp.sum(attn_probs * grad_prob, axis=-1, keepdims=True))
    scaled = (grad_score * temper).astype(jnp.bfloat16)
    grad_query = jnp.einsum("ghnm,gmhd->gnhd", scaled, key_rows, preferred_element_type=jnp.float32)
    grad_key = jnp.einsum("ghnm,gnhd->gmhd", scaled, query_rows, preferred_element_type=jnp.float32)
    grad_value = jnp.einsum(
        "ghnm,gnhd->gmhd", probs_low, grad_att, preferred_element_type=jnp.float32
    )
    grad_rows = (
        jnp.stack([grad_query, grad_key, grad_value], axis=2)
        .astype(jnp.bfloat16)
        .reshape(groups * WIN, 3 * C)
    )
    weight_qkv = jnp.einsum("tc,te->ce", flattened, grad_rows, preferred_element_type=jnp.float32)
    grad_shifted = jnp.einsum(
        "te,ce->tc", grad_rows, w_qkv, preferred_element_type=jnp.float32
    ).astype(jnp.bfloat16)
    return (grad_shifted.reshape(groups, WIN, C), weight_qkv, grad_proj, grad_score)


def body(attn_input, out_grad, w_qkv, w_proj, bias_table, mask_ids, valid_rows):
    levels, lat_rows, lon_cols, channels = attn_input.shape
    moved_input, moved_grad = displace([attn_input, out_grad], -1)
    shifted = to_windows(moved_input)
    grads_y = to_windows(moved_grad)
    anchor = jnp.arange(lat_rows, dtype=jnp.int32) + lax.axis_index("lat") * lat_rows + WLAT // 2
    usable = jnp.broadcast_to((anchor < valid_rows[0])[None, :, None], (levels, lat_rows, lon_cols))
    regions = to_windows(mask_ids)
    usable_win = to_windows(usable)
    allowed = (regions[..., :, None] == regions[..., None, :]) & usable_win[..., None, :]
    allowed = allowed | jnp.eye(WIN, dtype=bool)
    bias_full = expand_bias(bias_table)
    level_wins, lat_wins, lon_wins = shifted.shape[:3]

    def regroup(windows):
        rotated = jnp.moveaxis(windows, 1, 0)
        return rotated.reshape((lat_wins, level_wins * lon_wins) + windows.shape[3:])

    def one_band(pieces):
        band_input, band_grads, band_mask, band_bias = pieces
        expanded = band_bias[:, None]
        expanded = expanded.reshape(level_wins * lon_wins, HEADS, WIN, WIN)
        grad_in, weight_qkv, weight_proj, grad_score = window_backward(
            band_input, band_grads, band_mask, expanded, w_qkv, w_proj
        )
        folded = fold_bias(
            jnp.sum(grad_score.reshape(level_wins, lon_wins, HEADS, WIN, WIN), axis=1)
        )
        return (grad_in, weight_qkv, weight_proj, folded)

    grad_in, weight_qkv, weight_proj, folded = lax.map(
        one_band,
        (regroup(shifted), regroup(grads_y), regroup(allowed), jnp.moveaxis(bias_full, 1, 0)),
    )
    grad_in = jnp.moveaxis(grad_in.reshape((lat_wins, level_wins, lon_wins, WIN, channels)), 0, 1)
    grad_input = displace([from_windows(grad_in, levels, lat_rows, lon_cols)], 1)[0]
    local_qkv = jnp.sum(weight_qkv, axis=0)
    local_proj = jnp.sum(weight_proj, axis=0)
    local_table = jnp.moveaxis(folded, 0, 1)
    total_qkv, total_proj = lax.psum((local_qkv, local_proj), ("lon", "lat"))
    grad_bias = lax.psum(local_table, "lon")
    cells = levels * lat_rows * lax.axis_size("lat") * lon_cols * lax.axis_size("lon")
    factor = cells ** (-0.5)
    return (grad_input, total_qkv * factor, total_proj * factor, grad_bias)


def solution(mesh):
    placed = (
        P("batch", "lat", "lon", None),
        P("batch", "lat", "lon", None),
        P(),
        P(),
        P(None, "lat", None, None, None, None, None, None),
        P("batch", "lat", "lon"),
        P("batch"),
    )
    return jax.shard_map(
        body,
        mesh=mesh,
        in_specs=placed,
        out_specs=(
            P("batch", "lat", "lon", None),
            P("batch", None),
            P("batch", None),
            P("batch", "lat", None, None, None, None, None, None),
        ),
        check_vma=False,
    )
```

profile of v0, /device:TPU:0, one launch (start us, length us, event | category | flops | bytes accessed | tf_op | source)
XLA Modules:
  0.0 402.5 jit_solution(8974184092676421896)
XLA Ops:
  7.2 1.2 slice.88
  8.4 1.0 slice.89
  9.4 1.0 slice.92
  10.5 1.0 slice.93
  11.5 0.2 fusion.28
  11.6 0.1 fusion.27
  11.8 5.1 %collective-permute-start = (bf16[2,8,6,6,192]{4,1,3,2,0:T(8,128)(2,1)S(1)}, bf16[2,8,6,6,192]{4,1,3,2,0:T(8,128)(2,1)S(1)}, u32[]{:S(2)}, u32[]{:S(2)}) collective-permute-start(bf16[2,8,6,6,192]{4,1,3,2,0:T(8,128)(2,1)S(1)} %pad_maximum_fusion.2), channel_id=1, source_target_pairs={{0,24},{8,0},{16,8},{24,16},{1,25},{9,1},{17,9},{25,17},{2,26},{10... | collective-permute-start | bytes 663560 | tf_op jit(solution)/shard_map/ppermute | solution.py:20
  16.9 14.9 %convolution_bitcast_fusion = f32[4,1,6,2,6,12,2,6,12]{8,7,4,6,3,2,0,5,1:T(8,128)} fusion(f32[4,6,2,2,6,6,23]{6,3,5,4,2,1,0:T(2,128)S(1)} %bitcast.102, s32[12,12]{1,0:T(8,128)S(1)} %subtract_add_fusion), kind=kOutput, calls=%fused_computation.2 | convolution fusion | flops 137358576 | bytes 2309184 | tf_op jit(solution)/shard_map/...hxyuvr,abr->...hxuayvb/dot_general | solution.py:38
  31.8 39.3 %copy.57 = f32[4,1,6,2,6,12,2,6,12]{5,4,3,8,7,6,2,0,1:T(8,128)} copy(f32[4,1,6,2,6,12,2,6,12]{8,7,4,6,3,2,0,5,1:T(8,128)} %convolution_bitcast_fusion) | data formatting | bytes 3981312 | tf_op jit(solution)/shard_map/while/body/jit(dynamic_index_in_dim)/squeeze | solution.py:187
  71.0 19.5 %reshape.130 = f32[4,6,144,144]{2,3,1,0:T(8,128)} reshape(f32[4,1,6,2,6,12,2,6,12]{5,4,3,8,7,6,2,0,1:T(8,128)} %copy.57) | data formatting | bytes 3981312 | tf_op jit(solution)/shard_map/while/body/jit(dynamic_index_in_dim)/squeeze | solution.py:187
  90.6 0.1 eq.61
  91.3 0.1 broadcast_in_dim.56
  91.4 0.1 and.17
  91.6 0.1 fusion.14
  91.7 0.1 fusion.25
  91.8 0.1 pad_maximum_fusion.3
  91.8 1.5 collective-permute-start.1
  93.3 0.9 and_or_fusion
  94.2 1.1 collective-permute-done.1
  95.3 0.1 pad_maximum_fusion.5
  95.4 0.1 copy.34
  95.5 0.1 reshape.123
  95.6 0.3 convolution_convert_fusion.2
  95.9 1.0 reshape.124
  97.0 0.1 copy.26
  97.0 0.1 reshape.120
  97.2 0.4 convolution_convert_fusion
  97.6 0.4 copy.27
  97.9 0.8 reshape.121
  98.7 0.5 fusion.41
  99.2 2.8 add_select_fusion
  102.1 2.8 fusion.43
  104.8 4.0 convolution_bitcast_fusion.2
  108.8 2.5 fusion.11
  111.3 6.2 %convolution_bitcast_fusion.3 = bf16[4,144,1,6,32]{1,4,3,0,2:T(8,128)(2,1)S(1)} fusion(bf16[4,144,1,6,32]{1,0,4,3,2:T(4,128)(2,1)S(1)} %get-tuple-element.48, f32[4,6,144,144]{2,3,1,0:T(8,128)} %fusion.11, f32[4,6,144,144]{2,3,1,0:T(8,128)} %get-tuple-element.63, f32[4,6,144]{2,1,0:T(8,128)S(1)} %get-tuple-element.62), kind=kOutput, calls=%fused_computation.16 | convolution fusion | flops 35337744 | bytes 4437504 | tf_op jit(solution)/shard_map/while/body/eval_jaxpr/ghnm,gnhd->gmhd/dot_general | solution.py:141
  117.5 6.2 %convolution_bitcast_fusion.4 = bf16[4,144,1,6,32]{1,4,3,0,2:T(8,128)(2,1)S(1)} fusion(bf16[4,144,1,6,32]{1,0,4,3,2:T(4,128)(2,1)S(1)} %get-tuple-element.49, f32[4,6,144,144]{2,3,1,0:T(8,128)} %fusion.11, f32[4,6,144,144]{2,3,1,0:T(8,128)} %get-tuple-element.63, f32[4,6,144]{2,1,0:T(8,128)S(1)} %get-tuple-element.62), kind=kOutput, calls=%fused_computation.17 | convolution fusion | flops 35337744 | bytes 4437504 | tf_op jit(solution)/shard_map/while/body/eval_jaxpr/ghnm,gmhd->gnhd/dot_general | solution.py:140
  123.7 0.3 maximum_convert_fusion
  124.0 1.0 copy.41
  125.1 0.8 convert_element_type.50
  125.8 0.4 convolution_convert_fusion.3
  126.2 0.1 slice.130
  126.3 1.2 fusion.44
  127.6 4.1 %fusion.7 = bf16[4,144,6,32]{1,3,2,0:T(8,128)(2,1)S(1)} fusion(bf16[4,144,1,6,32]{1,0,4,3,2:T(4,128)(2,1)S(1)} %get-tuple-element.47, f32[4,6,144]{2,1,0:T(8,128)S(1)} %copy-done.7, f32[4,6,144,144]{2,3,1,0:T(8,128)} %copy-done.2), kind=kOutput, calls=%fused_computation.19 | convolution fusion | flops 33457680 | bytes 2446848 | tf_op jit(solution)/shard_map/while/body/eval_jaxpr/ghnm,gmhd->gnhd/dot_general | solution.py:127
  131.6 8.0 %subtract_multiply_fusion = f32[4,6,144,144]{2,3,1,0:T(8,128)} fusion(f32[4,6,144,144]{2,3,1,0:T(8,128)} %fusion.11, f32[4,6,144,144]{2,3,1,0:T(8,128)} %get-tuple-element.63, f32[4,6,144]{2,1,0:T(8,128)S(1)} %copy-done.7), kind=kOutput, calls=%fused_computation.4 | output fusion | flops 2491919 | bytes 5985792 | tf_op jit(solution)/shard_map/while/body/eval_jaxpr/sub | solution.py:138
  139.6 0.1 copy.42
  139.7 0.1 copy.43
  139.9 0.1 slice.110
  140.0 0.1 slice_bitcast_fusion
  140.1 0.1 collective-permute-start.2
  140.1 0.3 copy.45
  140.4 0.2 reshape.125
  140.7 0.9 fusion.45
  141.6 18.4 %reshape.131 = f32[4,6,2,6,12,2,6,12]{4,3,2,7,6,5,1,0:T(8,128)} reshape(f32[4,6,144,144]{2,3,1,0:T(8,128)} %subtract_multiply_fusion) | data formatting | bytes 3981312 | tf_op jit(solution)/shard_map/while/body/eval_jaxpr/reshape | solution.py:45
  160.0 38.2 %copy.47 = f32[4,6,2,6,12,2,6,12]{7,6,4,5,3,2,1,0:T(8,128)} copy(f32[4,6,2,6,12,2,6,12]{4,3,2,7,6,5,1,0:T(8,128)} %reshape.131) | data formatting | bytes 3981312 | tf_op jit(solution)/shard_map/while/body/eval_jaxpr/reshape | solution.py:45
  198.4 0.1 fusion.24
  198.4 6.4 %collective-permute-start.3 = (bf16[1,8,3,12,192]{4,3,2,1,0:T(8,128)(2,1)S(1)}, bf16[1,8,3,12,192]{4,3,2,1,0:T(8,128)(2,1)S(1)}, u32[]{:S(2)}, u32[]{:S(2)}) collective-permute-start(bf16[1,8,3,12,192]{4,3,2,1,0:T(8,128)(2,1)S(1)} %fusion.24), channel_id=1, source_target_pairs={{0,2},{2,4},{4,6},{1,3},{3,5},{5,7},{8,10},{10,12},{12,14},{9,11},... | collective-permute-start | bytes 331784 | tf_op jit(solution)/shard_map/ppermute | solution.py:26
  204.8 22.9 %convolution_bitcast_fusion.1 = f32[4,1,6,2,2,6,6,23]{7,6,4,5,3,2,0,1:T(8,128)} fusion(f32[4,6,2,6,12,2,6,12]{7,6,4,5,3,2,1,0:T(8,128)} %copy.47, s32[12,12]{1,0:T(8,128)S(1)} %subtract_add_fusion), kind=kOutput, calls=%fused_computation.13 | convolution fusion | flops 137358576 | bytes 2309184 | tf_op jit(solution)/shard_map/while/body/eval_jaxpr/...hxuayvb,abr->...hxyuvr/dot_general | solution.py:46
  227.7 0.1 fusion.10
  227.9 0.9 copy.48
  228.7 66.1 %all-reduce.6.cloned.1.call-done = (f32[192,576]{1,0:T(8,128)}, f32[192,192]{1,0:T(8,128)}) async-done(((f32[192,576]{1,0:T(8,128)}, f32[192,192]{1,0:T(8,128)}), (f32[192,576]{1,0:T(8,128)}, f32[192,192]{1,0:T(8,128)})) %all-reduce.6.cloned.1.call-update) | async-done | bytes 589840 | tf_op jit(solution)/shard_map/psum | solution.py:196
  294.8 1.6 broadcast_multiply_fusion.1
  296.4 1.9 broadcast_multiply_fusion
  298.3 93.6 %all-reduce.4.cloned.1.call-done = f32[4,1,6,2,2,6,6,23]{7,6,4,5,3,2,0,1:T(8,128)} async-done(((f32[4,1,6,2,2,6,6,23]{7,6,4,5,3,2,0,1:T(8,128)}), f32[4,1,6,2,2,6,6,23]{7,6,4,5,3,2,0,1:T(8,128)}) %all-reduce.4.cloned.1.call-update) | async-done | bytes 317968 | tf_op jit(solution)/shard_map/psum | solution.py:197
  391.8 3.8 copy.49
  (37 shorter events, 0.4 us)
Async XLA Ops:
  7.2 90.0 %copy-start = (bf16[192,576]{1,0:T(8,128)(2,1)S(1)}, bf16[192,576]{1,0:T(8,128)(2,1)}, u32[]{:S(2)}) copy-start(bf16[192,576]{1,0:T(8,128)(2,1)} %param.9) | copy-start | bytes 663556
  7.2 9.7 %copy-start.3 = (f32[4,1,6,2,2,6,6,23]{7,4,6,5,3,2,1,0:T(2,128)S(1)}, f32[4,1,6,2,2,6,6,23]{7,4,6,5,3,2,1,0:T(2,128)}, u32[]{:S(2)}) copy-start(f32[4,1,6,2,2,6,6,23]{7,4,6,5,3,2,1,0:T(2,128)} %param.11) | copy-start | bytes 953860
  7.2 287.6 %all-reduce.6.cloned.1.call-start = ((), (), s32[]{:S(2)}) async-start(), calls=%async_computation.1 | async-start | bytes 1376256 | tf_op jit(solution)/shard_map/psum | solution.py:196
  11.8 79.7 %collective-permute-start = (bf16[2,8,6,6,192]{4,1,3,2,0:T(8,128)(2,1)S(1)}, bf16[2,8,6,6,192]{4,1,3,2,0:T(8,128)(2,1)S(1)}, u32[]{:S(2)}, u32[]{:S(2)}) collective-permute-start(bf16[2,8,6,6,192]{4,1,3,2,0:T(8,128)(2,1)S(1)} %pad_maximum_fusion.2), channel_id=1, source_target_pairs={{0,24},{8,0},{16,8},{24,16},{1,25},{9,1},{17,9},{25,17},{2,26},{10... | collective-permute-start | bytes 663560 | tf_op jit(solution)/shard_map/ppermute | solution.py:20
  71.0 19.5 %copy-start.8 = (s32[8,6,12]{2,0,1:T(8,128)S(1)}, s32[8,6,12]{2,0,1:T(8,128)}, u32[]{:S(2)}) copy-start(s32[8,6,12]{2,0,1:T(8,128)} %param.12) | copy-start | bytes 6916
  90.6 5.0 %copy-start.5 = (bf16[192,192]{1,0:T(8,128)(2,1)S(1)}, bf16[192,192]{1,0:T(8,128)(2,1)}, u32[]{:S(2)}) copy-start(bf16[192,192]{1,0:T(8,128)(2,1)} %param.10) | copy-start | bytes 221188
  91.8 3.5 collective-permute-start.1
  102.0 2.8 copy-start.2
  102.0 2.8 copy-start.4
  104.8 12.7 %copy-start.6 = (f32[4,6,144]{2,1,0:T(8,128)}, f32[4,6,144]{2,1,0:T(8,128)S(1)}, u32[]{:S(2)}) copy-start(f32[4,6,144]{2,1,0:T(8,128)S(1)} %get-tuple-element.62) | copy-start | bytes 41476
  124.0 3.5 copy-start.7
  140.1 58.3 %collective-permute-start.2 = (bf16[1,8,6,6,192]{4,3,2,1,0:T(8,128)(2,1)S(1)}, bf16[1,8,6,6,192]{4,3,2,1,0:T(8,128)(2,1)S(1)}, u32[]{:S(2)}, u32[]{:S(2)}) collective-permute-start(bf16[1,8,6,6,192]{4,3,2,1,0:T(8,128)(2,1)S(1)} %get-tuple-element.50), channel_id=1, source_target_pairs={{0,8},{8,16},{16,24},{24,0},{1,9},{9,17},{17,25},{25,1},{2,10},{10... | collective-permute-start | bytes 331784 | tf_op jit(solution)/shard_map/ppermute | solution.py:20
  198.3 193.5 %all-reduce.4.cloned.1.call-start = ((), (), s32[]{:S(2)}) async-start(), calls=%async_computation | async-start | bytes 4718592 | tf_op jit(solution)/shard_map/psum | solution.py:197
  198.4 29.3 %collective-permute-start.3 = (bf16[1,8,3,12,192]{4,3,2,1,0:T(8,128)(2,1)S(1)}, bf16[1,8,3,12,192]{4,3,2,1,0:T(8,128)(2,1)S(1)}, u32[]{:S(2)}, u32[]{:S(2)}) collective-permute-start(bf16[1,8,3,12,192]{4,3,2,1,0:T(8,128)(2,1)S(1)} %fusion.24), channel_id=1, source_target_pairs={{0,2},{2,4},{4,6},{1,3},{3,5},{5,7},{8,10},{10,12},{12,14},{9,11},... | collective-permute-start | bytes 331784 | tf_op jit(solution)/shard_map/ppermute | solution.py:26
  227.7 167.9 %copy-start.1 = (bf16[192,576]{1,0:T(8,128)(2,1)S(1)}, bf16[192,576]{1,0:T(8,128)(2,1)}, u32[]{:S(2)}) copy-start(bf16[192,576]{1,0:T(8,128)(2,1)} %param.9) | copy-start | bytes 663556
Sparse Core Ops, SparseCore 0:
  198.4 96.3 all-reduce.5
  297.2 94.6 all-reduce.3
where the time goes:
time: 405 us; the launch traced here: 402 us
  waiting for transfers between devices  161 us (40%)
  local copies, waits for them, and re-layouts  131 us (32%)
  matrix products  66.7 us (16%)
  other arithmetic  16.3 us (4%)
  between operations  15.1 us (4%)
  starting transfers between devices  13.1 us (3%)
    psum x1, waiting for transfers between devices, body(): grad_bias = lax.psum(local_table, 'lon')  93.6 us
    psum x1, waiting for transfers between devices, body(): total_qkv, total_proj = lax.psum((local_qkv, local_proj), ('lon', 'lat'))  66.1 us
    squeeze x2, local copies, waits for them, and re-layouts, body(): lax.map(one_band, (regroup(shifted), regroup(grads_y), regroup(allowed),...  58.8 us
    reshape x2, local copies, waits for them, and re-layouts, fold_bias(): grads.reshape(grads.shape[:-3] + (HEADS, WZ, WLAT, WLON, WZ, WLAT, WLON))  56.7 us
    dot_general x1, matrix products, fold_bias(): jnp.einsum('...hxuayvb,abr->...hxyuvr', divided, lon_table(), precision=l...  22.9 us
    dot_general x1, matrix products, expand_bias(): jnp.einsum('...hxyuvr,abr->...hxuayvb', folded, lon_table(), precision=la...  14.9 us
  transfers between devices with their start and end apart: 6, of which 3 were waited for; matrix products, arithmetic and copies ran while one was open for 40% of the time, Pallas kernels for 0%

commit v1 on v0

--- a/solution.py
+++ b/solution.py
@@ -1,6 +1,11 @@
+import functools
+
 import jax
 import jax.numpy as jnp
+import numpy as np
 from jax import lax
+from jax.experimental import pallas as pl
+from jax.experimental.pallas import tpu as pltpu
 from jax.sharding import PartitionSpec as P
 
 C = 192
@@ -199,6 +204,354 @@
     factor = cells ** (-0.5)
     return (grad_input, total_qkv * factor, total_proj * factor, grad_bias)
 
+BANDS = 16
+PAD = 48
+COLS = 16
+
+
+def place_maps():
+    send = np.zeros((4 * PAD, WZ * WLAT * COLS), np.float32)
+    order = np.zeros((WIN, 4 * PAD), np.float32)
+    for a in range(WZ):
+        for b in range(WLAT // 2):
+            for c in range(WLON // 2):
+                for part in range(4):
+                    low_row, low_col = part // 2, part % 2
+                    spot = part * PAD + a * 18 + b * 6 + c
+                    row = b + (0 if low_row else 3)
+                    col = c + (0 if low_col else 6)
+                    send[spot, (a * WLAT + row) * COLS + col] = 1.0
+                    win_row = b + (3 if low_row else 0)
+                    win_col = c + (6 if low_col else 0)
+                    order[win_col * 12 + a * WLAT + win_row, spot] = 1.0
+    return send, order
+
+
+def bias_map():
+    spread = np.zeros((276, 384), np.float32)
+    for pair in range(12):
+        for d in range(23):
+            spread[pair * 23 + d, (22 - d) * 12 + pair] = 1.0
+    return spread
+
+
+def dot_nn(a, b):
+    return lax.dot_general(a, b, (((1,), (0,)), ((), ())), preferred_element_type=jnp.float32)
+
+
+def dot_nt(a, b):
+    return lax.dot_general(a, b, (((1,), (1,)), ((), ())), preferred_element_type=jnp.float32)
+
+
+def dot_tn(a, b):
+    return lax.dot_general(a, b, (((0,), (0,)), ((), ())), preferred_element_type=jnp.float32)
+
+
+def kernel(
+    factor, x_ref, g_ref, wq_ref, wp_ref, tab_ref, idr_ref, idc_ref,
+    p1_ref, p1t_ref, p2_ref, p2t_ref, gm_ref, gmt_ref,
+    out_x, out_w, out_p, out_b,
+    xs, sb, rb, hs, hr, bias, tp, fold, dsr, xa, ga, aa, gr, dw,
+    ws, wr, wl, wm, wf, wg, bs, br, bg, bo,
+    halo_send, halo_recv, back_send, back_recv, bsum_send, bsum_recv, ball_send, ball_recv,
+    wa_send, wa_recv, wb_send, wb_recv, wc_send, wc_recv, wd_send, wd_recv,
+):
+    f32, bf16 = jnp.float32, jnp.bfloat16
+    lon, lat = lax.axis_index("lon"), lax.axis_index("lat")
+    nl, nt = 4, 4
+
+    def at(dlon, dlat):
+        return {"lon": lax.rem(lon + dlon + nl, nl), "lat": lax.rem(lat + dlat + nt, nt)}
+
+    def remote(src, dst, send, recv, where):
+        return pltpu.make_async_remote_copy(
+            src_ref=src, dst_ref=dst, send_sem=send, recv_sem=recv,
+            device_id=where, device_id_type=pl.DeviceIdType.MESH,
+        )
+
+    barrier = pltpu.get_barrier_semaphore()
+    friends = [(1, 0), (2, 0), (3, 0), (0, 1), (0, 2), (0, 3), (1, 1), (-1, -1)]
+    for dlon, dlat in friends:
+        pl.semaphore_signal(
+            barrier, inc=1, device_id=at(dlon, dlat), device_id_type=pl.DeviceIdType.MESH
+        )
+
+    xs[...] = jnp.zeros_like(xs)
+    for arr, ref in enumerate((x_ref, g_ref)):
+        for z in range(8):
+            for r in range(6):
+                xs[arr, z, COLS * r : COLS * r + 12, :] = ref[z, r]
+    p1 = p1_ref[...]
+    for i in range(4):
+        for arr in range(2):
+            block = jnp.concatenate([xs[arr, (2 * i + 1) % 8], xs[arr, (2 * i + 2) % 8]], axis=0)
+            cut = dot_nn(p1, block).astype(bf16)
+            rb[0, arr, i] = cut[0:PAD]
+            for part in range(1, 4):
+                sb[part - 1, arr, i] = cut[part * PAD : (part + 1) * PAD]
+    pl.semaphore_wait(barrier, len(friends))
+    halo = [
+        remote(sb.at[n], rb.at[n + 1], halo_send.at[n], halo_recv.at[n], at(*where))
+        for n, where in enumerate(((-1, 0), (0, -1), (-1, -1)))
+    ]
+    for copy in halo:
+        copy.start()
+
+    def expand(i, carry):
+        table = tab_ref[i]
+        top = table.astype(bf16)
+        rest = table - top.astype(f32)
+        mid = rest.astype(bf16)
+        low = (rest - mid.astype(f32)).astype(bf16)
+        spread = gm_ref[...]
+        tp[...] = dot_nn(top, spread) + dot_nn(mid, spread) + dot_nn(low, spread)
+        for h in range(HEADS):
+            for c in range(12):
+                bias[i, h, 12 * c : 12 * c + 12, :] = tp[
+                    16 * h : 16 * h + 12, 12 * (11 - c) : 12 * (11 - c) + WIN
+                ]
+        return carry
+
+    lax.fori_loop(0, 4, expand, 0)
+    for n in range(16):
+        ws[n] = jnp.zeros((16, 768), bf16)
+    for copy in halo:
+        copy.wait()
+
+    spot = lax.broadcasted_iota(jnp.int32, (1, 4 * PAD), 1)
+    far = spot >= 2 * PAD
+    last_row = lat == nt - 1
+    first_row = lat == 0
+    p2 = p2_ref[...] * jnp.where(far & last_row, 0.0, 1.0).astype(bf16)
+    p1t = p1t_ref[...] * jnp.where(far & first_row, 0.0, 1.0).astype(bf16)
+    rows = lax.broadcasted_iota(jnp.int32, (WIN, WIN), 0)
+    cols = lax.broadcasted_iota(jnp.int32, (WIN, WIN), 1)
+    same = rows == cols
+    temper = HEAD_DIM ** (-0.5)
+
+    def bias_copy(s):
+        w = lax.rem(lon + 1 + s, nl)
+        return remote(bs.at[w], br.at[s], bsum_send.at[s], bsum_recv.at[s], at(1 + s, 0))
+
+    def window(s, carry):
+        w = lax.rem(lon + 1 + s, nl)
+        x4 = jnp.concatenate([rb[part, 0, w] for part in range(4)], axis=0)
+        g4 = jnp.concatenate([rb[part, 1, w] for part in range(4)], axis=0)
+        x = dot_nn(p2, x4).astype(bf16)
+        g = dot_nn(p2, g4).astype(bf16)
+        xa[w] = x
+        ga[w] = g
+        qkv = dot_nn(x, wq_ref[...]).astype(bf16)
+        gatt = dot_nt(g, wp_ref[...]).astype(bf16)
+        allowed = (idc_ref[w] == idr_ref[w]) | same
+        fold[...] = jnp.zeros_like(fold)
+        for h in range(HEADS):
+            lo = HEAD_DIM * h
+            q = qkv[:, lo : lo + 32]
+            k = qkv[:, C + lo : C + lo + 32]
+            v = qkv[:, 2 * C + lo : 2 * C + lo + 32]
+            go = gatt[:, lo : lo + 32]
+            scores = dot_nt(q, k) * temper + bias[w, h]
+            scores = jnp.where(allowed, scores, masked_score)
+            power = jnp.exp(scores - jnp.max(scores, axis=-1, keepdims=True))
+            probs = power / jnp.sum(power, axis=-1, keepdims=True)
+            low = probs.astype(bf16)
+            aa[w, :, lo : lo + 32] = dot_nn(low, v).astype(bf16)
+            gp = dot_nt(go, v)
+            gs = probs * (gp - jnp.sum(probs * gp, axis=-1, keepdims=True))
+            dsr[h] = gs
+            scaled = (gs * temper).astype(bf16)
+            gr[w, :, lo : lo + 32] = dot_nn(scaled, k).astype(bf16)
+            gr[w, :, C + lo : C + lo + 32] = dot_tn(scaled, q).astype(bf16)
+            gr[w, :, 2 * C + lo : 2 * C + lo + 32] = dot_tn(low, go).astype(bf16)
+            for c in range(12):
+                off = 12 * (11 - c)
+                fold[16 * h : 16 * h + 12, off : off + WIN] += dsr[h, 12 * c : 12 * c + 12, :]
+        back = dot_nt(gr[w], wq_ref[...]).astype(bf16)
+        cut = dot_nn(p2t_ref[...], back).astype(bf16)
+        for part in range(4):
+            hs[part, w] = cut[part * PAD : (part + 1) * PAD]
+        bs[w] = dot_nn(fold[...].astype(bf16), gmt_ref[...]).astype(bf16)
+
+        @pl.when(s < 3)
+        def _():
+            bias_copy(s).start()
+
+        return carry
+
+    lax.fori_loop(0, 4, window, 0)
+
+    home = [
+        remote(hs.at[n + 1], hr.at[n], back_send.at[n], back_recv.at[n], at(*where))
+        for n, where in enumerate(((1, 0), (0, 1), (1, 1)))
+    ]
+    for copy in home:
+        copy.start()
+
+    dw[:, :576] = dot_tn(xa[...].reshape(576, C), gr[...].reshape(576, 576))
+    dw[:, 576:] = dot_tn(aa[...].reshape(576, C), ga[...].reshape(576, C))
+    for n in range(16):
+        ws[n, 0:12, :] = dw[12 * n : 12 * n + 12, :].astype(bf16)
+    wa = []
+    for d in range(1, 4):
+        to = lax.rem(lat + d, nt)
+        wa.append(
+            remote(ws.at[pl.ds(4 * to, 4)], wr.at[d - 1], wa_send.at[d - 1], wa_recv.at[d - 1], at(0, d))
+        )
+    for copy in wa:
+        copy.start()
+
+    for s in range(3):
+        bias_copy(s).wait()
+    total = bs[lon].astype(f32)
+    for s in range(3):
+        total = total + br[s].astype(f32)
+    bg[...] = total.astype(bf16)
+    ball = [
+        remote(bg, bo.at[lon], ball_send.at[d - 1], ball_recv.at[d - 1], at(d, 0))
+        for d in range(1, 4)
+    ]
+    for copy in ball:
+        copy.start()
+
+    for copy in wa:
+        copy.wait()
+    part_sum = ws[pl.ds(4 * lat, 4)].astype(f32)
+    for d in range(3):
+        part_sum = part_sum + wr[d].astype(f32)
+    wl[...] = part_sum.astype(bf16)
+    wb = []
+    for d in range(1, 4):
+        to = lax.rem(lon + d, nl)
+        wb.append(
+            remote(wl.at[to], wm.at[d - 1], wb_send.at[d - 1], wb_recv.at[d - 1], at(d, 0))
+        )
+    for copy in wb:
+        copy.start()
+
+    for copy in home:
+        copy.wait()
+    for i in range(4):
+        y4 = jnp.concatenate([hs[0, i]] + [hr[n, i] for n in range(3)], axis=0)
+        y = dot_nn(p1t, y4).astype(bf16)
+        for a in range(2):
+            z = (2 * i + 1 + a) % 8
+            for r in range(6):
+                row = (a * 6 + r) * COLS
+                out_x[z, r] = y[row : row + 12]
+
+    for copy in wb:
+        copy.wait()
+    mine = wl[lon].astype(f32)
+    for d in range(3):
+        mine = mine + wm[d].astype(f32)
+    wf[...] = mine.astype(bf16)
+    wg[4 * lat + lon] = wf[...]
+    wc = [
+        remote(wf, wg.at[4 * lat + lon], wc_send.at[d - 1], wc_recv.at[d - 1], at(d, 0))
+        for d in range(1, 4)
+    ]
+    for copy in wc:
+        copy.start()
+    for copy in wc:
+        copy.wait()
+    own = wg.at[pl.ds(4 * lat, 4)]
+    wd = [
+        remote(own, own, wd_send.at[d - 1], wd_recv.at[d - 1], at(0, d))
+        for d in range(1, 4)
+    ]
+    for copy in wd:
+        copy.start()
+
+    for copy in ball:
+        copy.wait()
+    bo[lon] = bg[...]
+    out_b[...] = bo[...].astype(f32)
+
+    for copy in wd:
+        copy.wait()
+    for n in range(16):
+        piece = wg[n].astype(f32) * factor
+        out_w[12 * n : 12 * n + 12, :] = piece[0:12, :576]
+        out_p[12 * n : 12 * n + 12, :] = piece[0:12, 576:]
+
+
+def fused_body(attn_input, out_grad, w_qkv, w_proj, bias_table, mask_ids, valid_rows):
+    f32, bf16 = jnp.float32, jnp.bfloat16
+    levels, lat_rows, lon_cols, _ = attn_input.shape
+    anchor = jnp.arange(lat_rows, dtype=jnp.int32) + lax.axis_index("lat") * lat_rows + WLAT // 2
+    usable = (anchor < valid_rows[0])[None, :, None]
+    keyed = jnp.where(usable, mask_ids, -1)
+
+    def ordered(ids):
+        return ids.reshape(4, 2, 6, 12).transpose(0, 3, 1, 2)
+
+    idc = ordered(mask_ids).reshape(4, WIN, 1)
+    idr = ordered(keyed).reshape(4, 1, WIN)
+    table = bias_table.reshape(4, 6, 2, 2, 6, 6, 23).transpose(0, 1, 2, 4, 3, 5, 6)
+    table = table.reshape(4, 6, 12, 276)
+    table = jnp.pad(table, ((0, 0), (0, 0), (0, 4), (0, 0))).reshape(4, 96, 276)
+    send, order = place_maps()
+    spread = bias_map()
+    maps = [jnp.asarray(m, bf16) for m in (send, send.T, order, order.T, spread, spread.T)]
+    cells = levels * lat_rows * lax.axis_size("lat") * lon_cols * lax.axis_size("lon")
+    vm = pltpu.VMEM
+    sem = pltpu.SemaphoreType.DMA((3,))
+    scratch = [
+        vm((2, 8, 96, C), bf16),
+        vm((3, 2, 4, PAD, C), bf16),
+        vm((4, 2, 4, PAD, C), bf16),
+        vm((4, 4, PAD, C), bf16),
+        vm((3, 4, PAD, C), bf16),
+        vm((4, HEADS, WIN, WIN), f32),
+        vm((96, 384), f32),
+        vm((96, 384), f32),
+        vm((HEADS, WIN, WIN), f32),
+        vm((4, WIN, C), bf16),
+        vm((4, WIN, C), bf16),
+        vm((4, WIN, C), bf16),
+        vm((4, WIN, 3 * C), bf16),
+        vm((C, 768), f32),
+        vm((16, 16, 768), bf16),
+        vm((3, 4, 16, 768), bf16),
+        vm((4, 16, 768), bf16),
+        vm((3, 16, 768), bf16),
+        vm((16, 768), bf16),
+        vm((16, 16, 768), bf16),
+        vm((4, 96, 276), bf16),
+        vm((3, 96, 276), bf16),
+        vm((96, 276), bf16),
+        vm((4, 96, 276), bf16),
+    ] + [sem] * 16
+    whole = pl.BlockSpec(memory_space=pltpu.VMEM)
+    grad_input, grad_qkv, grad_proj, folded = pl.pallas_call(
+        functools.partial(kernel, cells ** (-0.5)),
+        out_shape=(
+            jax.ShapeDtypeStruct((8, 6, 12, C), bf16),
+            jax.ShapeDtypeStruct((C, 3 * C), f32),
+            jax.ShapeDtypeStruct((C, C), f32),
+            jax.ShapeDtypeStruct((4, 96, 276), f32),
+        ),
+        in_specs=[whole] * 13,
+        out_specs=[whole] * 4,
+        scratch_shapes=scratch,
+        compiler_params=pltpu.CompilerParams(
+            collective_id=0, has_side_effects=True, vmem_limit_bytes=48 * 1024 * 1024
+        ),
+    )(attn_input, out_grad, w_qkv, w_proj, table, idr, idc, *maps)
+    folded = folded.reshape(4, 6, 16, 276)[:, :, :12].reshape(4, 6, 2, 6, 2, 6, 23)
+    grad_bias = folded.transpose(0, 1, 2, 4, 3, 5, 6)[:, None]
+    return grad_input, grad_qkv, grad_proj, grad_bias
+
+
+def fitting_body(attn_input, *others):
+    tuned = (
+        lax.axis_size("lon") == 4
+        and lax.axis_size("lat") == 4
+        and attn_input.shape == (8, 6, 12, C)
+    )
+    return (fused_body if tuned else body)(attn_input, *others)
+
 
 def solution(mesh):
     placed = (
@@ -211,7 +564,7 @@
         P("batch"),
     )
     return jax.shard_map(
-        body,
+        fitting_body,
         mesh=mesh,
         in_specs=placed,
         out_specs=(

time: 405 us -> 73.2 us (0.18)
  waiting for transfers between devices: 161 us -> 0 us
  local copies, waits for them, and re-layouts: 131 us -> 13.7 us
  matrix products: 66.7 us -> 0 us
  Pallas kernels: 0 us -> 56.4 us
  other arithmetic: 16.3 us -> 0.82 us
  between operations: 15.1 us -> 1.59 us
  starting transfers between devices: 13.1 us -> 0 us
    psum x2 -> x0, waiting for transfers between devices: 160 us -> none  [the longest x1 93.6 us: body(): grad_bias = lax.psum(local_table, 'lon')]
    dot_general x13 -> x0, matrix products: 66.7 us -> none  [the longest x1 22.9 us: fold_bias(): jnp.einsum('...hxuayvb,abr->...hxyuvr', divided, lon_table(), precision=l...]
    squeeze x4 -> x0, local copies, waits for them, and re-layouts: 58.8 us -> none  [the longest x2 58.8 us: body(): lax.map(one_band, (regroup(shifted), regroup(grads_y), regroup(allowed),...]
    reshape x7 -> x5, local copies, waits for them, and re-layouts: 59 us -> 2.51 us  [the longest x1 1.21 us: fused_body(): folded.reshape(4, 6, 16, 276)[:, :, :12].reshape(4, 6, 2, 6, 2, 6, 23)]
    pallas_call x0 -> x1, Pallas kernels: none -> 56.4 us  [fused_body(): pl.pallas_call(functools.partial(kernel, cells ** (-0.5)), out_shape=(jax...]
    ppermute x4 -> x0, starting transfers between devices: 13 us -> none  [the longest x2 7.86 us: shifted_2(): return lax.ppermute(shard, axis, pairs)]
    sub x2 -> x0, other arithmetic: 10.8 us -> none  [the longest x1 7.98 us: window_backward(): grad_prob - jnp.sum(attn_probs * grad_prob, axis=-1, keepdims=True)]
    unnamed x22 -> x27, local copies, waits for them, and re-layouts: 4.74 us -> 11.1 us
  transfers between devices with their start and end apart: 6 -> 0, of which waited for: 3 -> 0; matrix products, arithmetic and copies ran while one was open for 40% -> 0% of each run, Pallas kernels for 0% -> 0%
where the time goes in v1:
time: 73.2 us; the launch traced here: 72.5 us
  Pallas kernels  56.4 us (77%)
  local copies, waits for them, and re-layouts  13.7 us (19%)
  between operations  1.59 us (2%)
  other arithmetic  0.82 us (1%)
    pallas_call x1, Pallas kernels, fused_body(): pl.pallas_call(functools.partial(kernel, cells ** (-0.5)), out_shape=(jax...  56.4 us
    unnamed x27, local copies, waits for them, and re-layouts  11.1 us

profile of v1, /device:TPU:0, one launch (start us, length us, event | category | flops | bytes accessed | tf_op | source)
XLA Modules:
  0.0 72.5 jit_solution(3632024708558494801)
XLA Ops:
  0.6 0.0 copy-start.8
  1.4 0.8 %broadcast_select_fusion = s32[8,6,12]{2,0,1:T(8,128)S(1)} fusion(s32[8,6,12]{2,0,1:T(8,128)} %param.18, pred[6]{0:T(512)(128)(4,1)S(1)} %add_compare_fusion), kind=kLoop, calls=%fused_computation | loop fusion | flops 576 | bytes 4614 | tf_op jit(solution)/shard_map/jit(_where)/select_n | solution.py:484
  2.2 0.1 copy.24
  2.4 0.1 reshape.50.idr_ref
  2.5 0.9 %copy.25 = s32[4,2,6,12]{2,1,3,0:T(2,128)S(1)} copy(s32[4,2,6,12]{3,1,0,2:T(2,128)} %bitcast.23) | data formatting | bytes 4608 | tf_op jit(solution)/shard_map/reshape | solution.py:487
  3.4 0.2 reshape.51.idc_ref
  3.5 1.0 %copy.26.x_ref = bf16[8,6,12,192]{3,2,1,0:T(8,128)(2,1)S(1)} copy(bf16[8,6,12,192]{3,0,2,1:T(8,128)(2,1)} %param.13) | data formatting | bytes 442368 | tf_op args[0]
  4.6 1.0 %copy.27.g_ref = bf16[8,6,12,192]{3,2,1,0:T(8,128)(2,1)S(1)} copy(bf16[8,6,12,192]{3,0,2,1:T(8,128)(2,1)} %param.14) | data formatting | bytes 442368 | tf_op args[1]
  5.6 0.0 copy-done.8
  5.6 1.8 %copy.35 = f32[4,6,2,6,2,6,23]{6,5,4,3,2,1,0:T(8,128)} copy(f32[4,6,2,6,2,6,23]{6,4,5,3,2,1,0:T(2,128)S(1)} %bitcast.20) | data formatting | bytes 635904
  7.4 0.0 copy-start
  7.4 0.0 copy-start.1
  7.4 0.0 copy-start.2
  7.4 0.0 copy-start.3
  7.4 0.0 copy-start.4
  7.4 0.0 copy-start.5
  7.4 0.0 copy-start.6
  7.4 0.0 copy-start.7
  7.4 2.5 %reshape.52 = f32[4,6,12,276]{3,2,1,0:T(8,128)S(1)} reshape(f32[4,6,2,6,2,6,23]{6,5,4,3,2,1,0:T(8,128)} %copy.35) | data formatting | bytes 635904
  10.0 0.0 copy-done
  10.1 0.0 copy-done.1
  10.1 0.0 copy-done.2
  10.1 0.0 copy-done.3
  10.1 0.0 copy-done.4
  10.1 0.0 copy-done.5
  10.1 0.0 copy-done.6
  10.1 0.0 copy-done.7
  10.1 56.4 %shard_map.156 = (bf16[8,6,12,192]{3,2,1,0:T(8,128)(2,1)S(1)}, f32[192,576]{1,0:T(8,128)S(1)}, f32[192,192]{1,0:T(8,128)S(1)}, f32[4,96,276]{2,1,0:T(8,128)S(1)}) custom-call(bf16[8,6,12,192]{3,2,1,0:T(8,128)(2,1)S(1)} %copy.26.x_ref, bf16[8,6,12,192]{3,2,1,0:T(8,128)(2,1)S(1)} %copy.27.g_ref, bf16[192,576]{1,0:T(8,128)(2,1)S(1)} %copy-done.1, ...), custom_call_target="tpu_custom_call" | custom-call | tf_op jit(solution)/shard_map/pallas_call | solution.py:527
  66.5 0.9 %copy.31 = bf16[8,6,12,192]{3,0,2,1:T(8,128)(2,1)} copy(bf16[8,6,12,192]{3,2,1,0:T(8,128)(2,1)S(1)} %get-tuple-element.16) | data formatting | bytes 442368
  67.4 0.3 copy.33
  67.7 1.2 %reshape.49 = f32[4,6,2,6,2,6,23]{6,5,4,0,3,2,1:T(8,128)S(1)} reshape(f32[4,6,12,276]{3,0,2,1:T(4,128)S(1)} %copy.33) | data formatting | bytes 635904 | tf_op jit(solution)/shard_map/reshape | solution.py:542
  68.9 2.1 %copy.32 = f32[4,1,6,2,2,6,6,23]{7,4,6,5,3,2,1,0:T(2,128)} copy(f32[4,1,6,2,2,6,6,23]{7,6,4,0,5,3,2,1:T(8,128)S(1)} %bitcast.19) | data formatting | bytes 635904
  71.1 0.8 %copy.40 = f32[192,576]{1,0:T(8,128)} copy(f32[192,576]{1,0:T(8,128)S(1)} %get-tuple-element.25) | data formatting | bytes 884736
  71.8 0.7 copy.41
  (2 shorter events, 0.1 us)
Async XLA Ops:
  0.6 5.0 %copy-start.8 = (f32[4,1,6,2,2,6,6,23]{7,4,6,5,3,2,1,0:T(2,128)S(1)}, f32[4,1,6,2,2,6,6,23]{7,4,6,5,3,2,1,0:T(2,128)}, u32[]{:S(2)}) copy-start(f32[4,1,6,2,2,6,6,23]{7,4,6,5,3,2,1,0:T(2,128)} %param.17) | copy-start | bytes 953860
  7.4 2.7 %copy-start = (bf16[384,276]{1,0:T(8,128)(2,1)S(1)}, bf16[384,276]{1,0:T(8,128)(2,1)}, u32[]{:S(2)}) copy-start(bf16[384,276]{1,0:T(8,128)(2,1)} %constant.32.clone.gmt_ref) | copy-start | bytes 635908
  7.4 2.7 %copy-start.1 = (bf16[192,576]{1,0:T(8,128)(2,1)S(1)}, bf16[192,576]{1,0:T(8,128)(2,1)}, u32[]{:S(2)}) copy-start(bf16[192,576]{1,0:T(8,128)(2,1)} %wq_ref.1) | copy-start | bytes 663556
  7.4 2.7 %copy-start.2 = (bf16[276,384]{1,0:T(8,128)(2,1)S(1)}, bf16[276,384]{1,0:T(8,128)(2,1)}, u32[]{:S(2)}) copy-start(bf16[276,384]{1,0:T(8,128)(2,1)} %constant.31.clone.gm_ref) | copy-start | bytes 635908
  7.4 2.7 %copy-start.3 = (bf16[192,192]{1,0:T(8,128)(2,1)S(1)}, bf16[192,192]{1,0:T(8,128)(2,1)}, u32[]{:S(2)}) copy-start(bf16[192,192]{1,0:T(8,128)(2,1)} %wp_ref.1) | copy-start | bytes 221188
  7.4 2.7 %copy-start.4 = (bf16[192,144]{1,0:T(8,128)(2,1)S(1)}, bf16[192,144]{1,0:T(8,128)(2,1)}, u32[]{:S(2)}) copy-start(bf16[192,144]{1,0:T(8,128)(2,1)} %constant.30.clone.p2t_ref) | copy-start | bytes 165892
  7.4 2.7 %copy-start.5 = (bf16[192,192]{1,0:T(8,128)(2,1)S(1)}, bf16[192,192]{1,0:T(8,128)(2,1)}, u32[]{:S(2)}) copy-start(bf16[192,192]{1,0:T(8,128)(2,1)} %constant.28.clone.p1t_ref) | copy-start | bytes 221188
  7.4 2.7 %copy-start.6 = (bf16[192,192]{1,0:T(8,128)(2,1)S(1)}, bf16[192,192]{1,0:T(8,128)(2,1)}, u32[]{:S(2)}) copy-start(bf16[192,192]{1,0:T(8,128)(2,1)} %constant.27.clone.p1_ref) | copy-start | bytes 221188
  7.4 2.7 %copy-start.7 = (bf16[144,192]{1,0:T(8,128)(2,1)S(1)}, bf16[144,192]{1,0:T(8,128)(2,1)}, u32[]{:S(2)}) copy-start(bf16[144,192]{1,0:T(8,128)(2,1)} %constant.29.clone.p2_ref) | copy-start | bytes 165892

commit v2 on v0

--- a/solution.py
+++ b/solution.py
@@ -1,6 +1,11 @@
+import functools
+
 import jax
 import jax.numpy as jnp
+import numpy as np
 from jax import lax
+from jax.experimental import pallas as pl
+from jax.experimental.pallas import tpu as pltpu
 from jax.sharding import PartitionSpec as P
 
 C = 192
@@ -199,6 +204,349 @@
     factor = cells ** (-0.5)
     return (grad_input, total_qkv * factor, total_proj * factor, grad_bias)
 
+def place_map():
+    order = np.zeros((576, 576), np.float32)
+    for i in range(4):
+        for c in range(12):
+            for a in range(2):
+                for b in range(6):
+                    order[i * WIN + c * 12 + a * 6 + b, b * 96 + c * 8 + (2 * i + a + 1) % 8] = 1.0
+    return order
+
+
+def bias_map():
+    spread = np.zeros((384, 384), np.float32)
+    for a in range(2):
+        for b in range(6):
+            for d in range(23):
+                spread[(2 * b + a) * 32 + d, (22 - d) * 12 + a * 6 + b] = 1.0
+    return spread
+
+
+def dot_nn(a, b):
+    return lax.dot_general(a, b, (((1,), (0,)), ((), ())), preferred_element_type=jnp.float32)
+
+
+def dot_nt(a, b):
+    return lax.dot_general(a, b, (((1,), (1,)), ((), ())), preferred_element_type=jnp.float32)
+
+
+def dot_tn(a, b):
+    return lax.dot_general(a, b, (((0,), (0,)), ((), ())), preferred_element_type=jnp.float32)
+
+
+def kernel(
+    factor, x_ref, g_ref, wq_ref, wp_ref, tab_ref, ids_ref,
+    pm_ref, pt_ref, gm_ref, gmt_ref,
+    out_x, out_w, out_p, out_b,
+    pk, sg, hs, og, bias, tabx, tp, fold, dsr, xa, ga, aa, gr, qa, ca, dw,
+    ws, wr1, w2, wr2, wl, wm, wf, wo, bs, br, bg, bo,
+    halo_send, halo_recv, back_send, back_recv, bsum_send, bsum_recv, ball_send, ball_recv,
+    wb_send, wb_recv, wc_send, wc_recv, pair_send, pair_recv,
+):
+    f32, bf16 = jnp.float32, jnp.bfloat16
+    lon, lat = lax.axis_index("lon"), lax.axis_index("lat")
+    nl, nt = 4, 4
+    core, far_y = lax.rem(lat, 2), lat // 2
+
+    def at(dlon, dlat):
+        return {"lon": lax.rem(lon + dlon + nl, nl), "lat": lax.rem(lat + dlat + nt, nt)}
+
+    def remote(src, dst, send, recv, where):
+        return pltpu.make_async_remote_copy(
+            src_ref=src, dst_ref=dst, send_sem=send, recv_sem=recv,
+            device_id=where, device_id_type=pl.DeviceIdType.MESH,
+        )
+
+    barrier = pltpu.get_barrier_semaphore()
+    friends = [(1, 0), (2, 0), (3, 0), (0, 1), (0, 2), (0, 3), (1, 1), (-1, -1)]
+    for dlon, dlat in friends:
+        pl.semaphore_signal(
+            barrier, inc=1, device_id=at(dlon, dlat), device_id_type=pl.DeviceIdType.MESH
+        )
+
+    pk[:, :, :, 0:C] = x_ref[...]
+    pk[:, :, :, C : 2 * C] = g_ref[...]
+    sg[0:3, 0] = pk[3:6, 1]
+    pl.semaphore_wait(barrier, len(friends))
+    halo = [
+        remote(pk.at[pl.ds(3, 3), 0], sg.at[pl.ds(0, 3), 1], halo_send.at[0], halo_recv.at[0], at(-1, 0)),
+        remote(pk.at[pl.ds(0, 3), 0], sg.at[pl.ds(3, 3), 1], halo_send.at[2], halo_recv.at[2], at(-1, -1)),
+        remote(pk.at[pl.ds(0, 3), 1], sg.at[pl.ds(3, 3), 0], halo_send.at[1], halo_recv.at[1], at(0, -1)),
+    ]
+    for copy in halo:
+        copy.start()
+
+    tabx[...] = jnp.zeros_like(tabx)
+    for p in range(12):
+        tabx[:, 32 * p : 32 * p + 23] = tab_ref[pl.ds(p, 288, stride=12), :]
+    table = tabx[...]
+    top = table.astype(bf16)
+    rest = table - top.astype(f32)
+    mid = rest.astype(bf16)
+    low_part = (rest - mid.astype(f32)).astype(bf16)
+    spread = gm_ref[...]
+    spreaded = dot_nn(top, spread) + dot_nn(mid, spread) + dot_nn(low_part, spread)
+    for i in range(4):
+        tp[i] = spreaded[72 * i : 72 * i + 72]
+
+    def expand(i, carry):
+        for h in range(HEADS):
+            for c in range(12):
+                bias[i, h, 12 * c : 12 * c + 12, :] = tp[
+                    i, 12 * h : 12 * h + 12, 12 * (11 - c) : 12 * (11 - c) + WIN
+                ]
+        return carry
+
+    lax.fori_loop(0, 4, expand, 0)
+    for n in range(4):
+        wl[n] = jnp.zeros((16, 768), bf16)
+    spot = lax.broadcasted_iota(jnp.int32, (1, 576), 1)
+    keep = jnp.where((spot >= 288) & (lat == nt - 1), 0.0, 1.0).astype(bf16)
+    pm = pm_ref[...] * keep
+    rows = lax.broadcasted_iota(jnp.int32, (WIN, WIN), 0)
+    cols = lax.broadcasted_iota(jnp.int32, (WIN, WIN), 1)
+    same = rows == cols
+    for copy in halo:
+        copy.wait()
+
+    both = dot_nn(pm, sg[...].reshape(576, 2 * C)).astype(bf16)
+    xs = both[:, :C]
+    gs_all = both[:, C:]
+    xa[...] = xs
+    ga[...] = gs_all
+    qkv_all = dot_nn(xs, wq_ref[...]).astype(bf16)
+    gatt_all = dot_nt(gs_all, wp_ref[...]).astype(bf16)
+    for i in range(4):
+        qa[i] = qkv_all[WIN * i : WIN * i + WIN]
+        ca[i] = gatt_all[WIN * i : WIN * i + WIN]
+    temper = HEAD_DIM ** (-0.5)
+    lane = lax.broadcasted_iota(jnp.int32, (WIN, 8), 1)
+
+    def bias_copy(s):
+        w = lax.rem(lon + 1 + s, nl)
+        return remote(bs.at[w], br.at[s], bsum_send.at[s], bsum_recv.at[s], at(1 + s, 0))
+
+    def window(s, carry):
+        w = lax.rem(lon + 1 + s, nl)
+        code = ids_ref[w]
+        usable = code >= 4
+        region = jnp.where(usable, code - 4, code)
+        hot = jnp.where(region == lane, 1.0, 0.0).astype(bf16)
+        keyed = jnp.where(usable & (region == lane), 1.0, 0.0).astype(bf16)
+        allowed = (dot_nt(hot, keyed) > 0.5) | same
+        fold[...] = jnp.zeros_like(fold)
+        for h in range(HEADS):
+            lo = HEAD_DIM * h
+            q = qa[w, :, lo : lo + 32]
+            k = qa[w, :, C + lo : C + lo + 32]
+            v = qa[w, :, 2 * C + lo : 2 * C + lo + 32]
+            go = ca[w, :, lo : lo + 32]
+            scores = dot_nt(q, k) * temper + bias[w, h]
+            scores = jnp.where(allowed, scores, masked_score)
+            power = jnp.exp(scores - jnp.max(scores, axis=-1, keepdims=True))
+            probs = power * (1.0 / jnp.sum(power, axis=-1, keepdims=True))
+            low = probs.astype(bf16)
+            aa[w, :, lo : lo + 32] = dot_nn(low, v).astype(bf16)
+            gp = dot_nt(go, v)
+            gs = probs * (gp - jnp.sum(probs * gp, axis=-1, keepdims=True))
+            dsr[h] = gs
+            scaled = (gs * temper).astype(bf16)
+            gr[w, :, lo : lo + 32] = dot_nn(scaled, k).astype(bf16)
+            gr[w, :, C + lo : C + lo + 32] = dot_tn(scaled, q).astype(bf16)
+            gr[w, :, 2 * C + lo : 2 * C + lo + 32] = dot_tn(low, go).astype(bf16)
+            for c in range(12):
+                off = 12 * (11 - c)
+                fold[12 * h : 12 * h + 12, off : off + WIN] += dsr[h, 12 * c : 12 * c + 12, :]
+        bs[w] = dot_nn(fold[...].astype(bf16), gmt_ref[...]).astype(bf16)
+
+        @pl.when(s < 3)
+        def _():
+            bias_copy(s).start()
+
+        return carry
+
+    lax.fori_loop(0, 4, window, 0)
+
+    grads = gr[...].reshape(576, 576)
+    dw[:, :576] = dot_tn(xa[...], grads)
+    dw[:, 576:] = dot_tn(aa[...].reshape(576, C), ga[...])
+    for n in range(4):
+        ws[n % 2, n // 2] = dw[48 * n : 48 * n + 48, :].astype(bf16)
+    mate = {"lat": lat + 1 - 2 * core}
+    first = remote(ws.at[1 - core], wr1, pair_send.at[0], pair_recv.at[0], mate)
+    first.start()
+
+    back = dot_nt(grads, wq_ref[...]).astype(bf16)
+    hs[...] = dot_nn(pt_ref[...], back).astype(bf16).reshape(6, 2, PAD, C)
+
+    first.wait()
+    w2[...] = (ws[core].astype(f32) + wr1[...].astype(f32)).astype(bf16)
+    across = {"lat": lax.rem(lat + 2, nt)}
+    second = remote(w2.at[1 - far_y], wr2, pair_send.at[1], pair_recv.at[1], across)
+    second.start()
+    home = [
+        remote(hs.at[pl.ds(0, 3), 1], og.at[pl.ds(3, 3), 0], back_send.at[0], back_recv.at[0], at(1, 0)),
+        remote(hs.at[pl.ds(3, 3), 1], og.at[pl.ds(0, 3), 0], back_send.at[2], back_recv.at[2], at(1, 1)),
+        remote(hs.at[pl.ds(3, 3), 0], og.at[pl.ds(0, 3), 1], back_send.at[1], back_recv.at[1], at(0, 1)),
+    ]
+
+    for s in range(3):
+        bias_copy(s).wait()
+    total = bs[lon].astype(f32)
+    for s in range(3):
+        total = total + br[s].astype(f32)
+    bg[...] = total.astype(bf16)
+
+    second.wait()
+    part_sum = w2[far_y].astype(f32) + wr2[...].astype(f32)
+    dw[0:48, :] = part_sum
+    for n in range(4):
+        wl[n, 0:12, :] = dw[12 * n : 12 * n + 12, :].astype(bf16)
+    wb = []
+    for d in range(1, 4):
+        to = lax.rem(lon + d, nl)
+        wb.append(
+            remote(wl.at[to], wm.at[d - 1], wb_send.at[d - 1], wb_recv.at[d - 1], at(d, 0))
+        )
+    for copy in wb:
+        copy.start()
+    for copy in home:
+        copy.start()
+    ball = [
+        remote(bg, bo.at[lon], ball_send.at[d - 1], ball_recv.at[d - 1], at(d, 0))
+        for d in range(1, 4)
+    ]
+
+    og[3:6, 1] = hs[0:3, 0]
+    bo[lon] = bg[...]
+    for copy in wb:
+        copy.wait()
+    mine = wl[lon].astype(f32)
+    for d in range(3):
+        mine = mine + wm[d].astype(f32)
+    wf[...] = mine.astype(bf16)
+    wo[core, far_y, lon] = wf[...]
+    wc = [
+        remote(wf, wo.at[core, far_y, lon], wc_send.at[d - 1], wc_recv.at[d - 1], at(d, 0))
+        for d in range(1, 4)
+    ]
+    for copy in wc:
+        copy.start()
+    for copy in ball:
+        copy.start()
+    for copy in wc:
+        copy.wait()
+    own = wo.at[core, far_y]
+    third = remote(own, own, pair_send.at[2], pair_recv.at[2], across)
+    third.start()
+
+    for copy in home:
+        copy.wait()
+    fill = jnp.where(lat == 0, 0.0, 1.0).astype(bf16)
+    out_x[0:3] = og[0:3] * fill
+    out_x[3:6] = og[3:6]
+
+    third.wait()
+    half = wo.at[core]
+    fourth = remote(half, half, pair_send.at[3], pair_recv.at[3], mate)
+    fourth.start()
+
+    for copy in ball:
+        copy.wait()
+    for i in range(4):
+        piece = bo[i].astype(f32)
+        for p in range(12):
+            out_b[pl.ds(864 * i + p, 72, stride=12), :] = piece[0:72, 32 * p : 32 * p + 23]
+
+    fourth.wait()
+    for n in range(16):
+        piece = wo[(n // 4) % 2, n // 8, n % 4].astype(f32) * factor
+        out_w[12 * n : 12 * n + 12, :] = piece[0:12, :576]
+        out_p[12 * n : 12 * n + 12, :] = piece[0:12, 576:]
+
+
+def fused_body(attn_input, out_grad, w_qkv, w_proj, bias_table, mask_ids, valid_rows):
+    f32, bf16 = jnp.float32, jnp.bfloat16
+    levels, lat_rows, lon_cols, _ = attn_input.shape
+    anchor = jnp.arange(lat_rows, dtype=jnp.int32) + lax.axis_index("lat") * lat_rows + WLAT // 2
+    usable = (anchor < valid_rows[0])[None, :, None]
+    codes = jnp.where(usable, mask_ids + 4, mask_ids)
+    codes = codes.reshape(4, 2, 6, 12).transpose(0, 3, 1, 2).reshape(4, WIN, 1)
+    table = bias_table.transpose(0, 1, 2, 3, 5, 6, 4, 7).reshape(3456, 23)
+
+    def turned(field):
+        return field.transpose(1, 2, 0, 3).reshape(6, 2, PAD, C)
+
+    order = place_map()
+    spread = bias_map()
+    maps = [jnp.asarray(m, bf16) for m in (order, order.T, spread, spread.T)]
+    cells = levels * lat_rows * lax.axis_size("lat") * lon_cols * lax.axis_size("lon")
+    vm = pltpu.VMEM
+    sem = pltpu.SemaphoreType.DMA((3,))
+    four = pltpu.SemaphoreType.DMA((4,))
+    scratch = [
+        vm((6, 2, PAD, 2 * C), bf16),
+        vm((6, 2, PAD, 2 * C), bf16),
+        vm((6, 2, PAD, C), bf16),
+        vm((6, 2, PAD, C), bf16),
+        vm((4, HEADS, WIN, WIN), f32),
+        vm((288, 384), f32),
+        vm((4, 72, 384), f32),
+        vm((80, 384), f32),
+        vm((HEADS, WIN, WIN), f32),
+        vm((576, C), bf16),
+        vm((576, C), bf16),
+        vm((4, WIN, C), bf16),
+        vm((4, WIN, 3 * C), bf16),
+        vm((4, WIN, 3 * C), bf16),
+        vm((4, WIN, C), bf16),
+        vm((C, 768), f32),
+        vm((2, 2, 48, 768), bf16),
+        vm((2, 48, 768), bf16),
+        vm((2, 48, 768), bf16),
+        vm((48, 768), bf16),
+        vm((4, 16, 768), bf16),
+        vm((3, 16, 768), bf16),
+        vm((16, 768), bf16),
+        vm((2, 2, 4, 16, 768), bf16),
+        vm((4, 80, 384), bf16),
+        vm((3, 80, 384), bf16),
+        vm((80, 384), bf16),
+        vm((4, 80, 384), bf16),
+    ] + [sem] * 12 + [four] * 2
+    whole = pl.BlockSpec(memory_space=pltpu.VMEM)
+    grad_input, grad_qkv, grad_proj, folded = pl.pallas_call(
+        functools.partial(kernel, cells ** (-0.5)),
+        out_shape=(
+            jax.ShapeDtypeStruct((6, 2, PAD, C), bf16),
+            jax.ShapeDtypeStruct((C, 3 * C), f32),
+            jax.ShapeDtypeStruct((C, C), f32),
+            jax.ShapeDtypeStruct((3456, 23), f32),
+        ),
+        in_specs=[whole] * 10,
+        out_specs=[whole] * 4,
+        scratch_shapes=scratch,
+        compiler_params=pltpu.CompilerParams(
+            collective_id=0, has_side_effects=True, vmem_limit_bytes=48 * 1024 * 1024
+        ),
+    )(turned(attn_input), turned(out_grad), w_qkv, w_proj, table, codes, *maps)
+    grad_input = grad_input.reshape(6, 12, 8, C).transpose(2, 0, 1, 3)
+    folded = folded.reshape(4, 1, 6, 2, 6, 6, 2, 23)
+    return grad_input, grad_qkv, grad_proj, folded.transpose(0, 1, 2, 3, 6, 4, 5, 7)
+
+
+def fitting_body(attn_input, *others):
+    tuned = (
+        lax.axis_size("lon") == 4
+        and lax.axis_size("lat") == 4
+        and attn_input.shape == (8, 6, 12, C)
+    )
+    return (fused_body if tuned else body)(attn_input, *others)
+
+
+PAD = 48
+
 
 def solution(mesh):
     placed = (
@@ -211,7 +559,7 @@
         P("batch"),
     )
     return jax.shard_map(
-        body,
+        fitting_body,
         mesh=mesh,
         in_specs=placed,
         out_specs=(

time: 405 us -> 66.8 us (0.16)
  waiting for transfers between devices: 161 us -> 0 us
  local copies, waits for them, and re-layouts: 131 us -> 11.6 us
  matrix products: 66.7 us -> 0 us
  Pallas kernels: 0 us -> 52.6 us
  other arithmetic: 16.3 us -> 0.82 us
  between operations: 15.1 us -> 1.32 us
  starting transfers between devices: 13.1 us -> 0 us
    psum x2 -> x0, waiting for transfers between devices: 160 us -> none  [the longest x1 93.6 us: body(): grad_bias = lax.psum(local_table, 'lon')]
    dot_general x13 -> x0, matrix products: 66.7 us -> none  [the longest x1 22.9 us: fold_bias(): jnp.einsum('...hxuayvb,abr->...hxyuvr', divided, lon_table(), precision=l...]
    squeeze x4 -> x0, local copies, waits for them, and re-layouts: 58.8 us -> none  [the longest x2 58.8 us: body(): lax.map(one_band, (regroup(shifted), regroup(grads_y), regroup(allowed),...]
    reshape x7 -> x2, local copies, waits for them, and re-layouts: 59 us -> 0.3 us  [fused_body(): codes = codes.reshape(4, 2, 6, 12).transpose(0, 3, 1, 2).reshape(4, WIN, 1)]
    pallas_call x0 -> x1, Pallas kernels: none -> 52.6 us  [fused_body(): pl.pallas_call(functools.partial(kernel, cells ** (-0.5)), out_shape=(jax...]
    ppermute x4 -> x0, starting transfers between devices: 13 us -> none  [the longest x2 7.86 us: shifted_2(): return lax.ppermute(shard, axis, pairs)]
    sub x2 -> x0, other arithmetic: 10.8 us -> none  [the longest x1 7.98 us: window_backward(): grad_prob - jnp.sum(attn_probs * grad_prob, axis=-1, keepdims=True)]
    unnamed x22 -> x20, local copies, waits for them, and re-layouts: 4.74 us -> 11.3 us
  transfers between devices with their start and end apart: 6 -> 0, of which waited for: 3 -> 0; matrix products, arithmetic and copies ran while one was open for 40% -> 0% of each run, Pallas kernels for 0% -> 0%
where the time goes in v2:
time: 66.8 us; the launch traced here: 66.3 us
  Pallas kernels  52.6 us (79%)
  local copies, waits for them, and re-layouts  11.6 us (17%)
  between operations  1.32 us (2%)
  other arithmetic  0.82 us (1%)
    pallas_call x1, Pallas kernels, fused_body(): pl.pallas_call(functools.partial(kernel, cells ** (-0.5)), out_shape=(jax...  52.6 us
    unnamed x20, local copies, waits for them, and re-layouts  11.3 us

profile of v2, /device:TPU:0, one launch (start us, length us, event | category | flops | bytes accessed | tf_op | source)
XLA Modules:
  0.0 66.3 jit_solution(2534793392126338143)
XLA Ops:
  1.3 0.8 %add_select_fusion = s32[8,6,12]{2,0,1:T(8,128)S(1)} fusion(s32[8,6,12]{2,0,1:T(8,128)} %param.16, pred[6]{0:T(512)(128)(4,1)S(1)} %add_compare_fusion), kind=kLoop, calls=%fused_computation | loop fusion | flops 1152 | bytes 4614 | tf_op jit(solution)/shard_map/jit(_where)/select_n | solution.py:474
  2.1 0.1 copy.17
  2.2 0.2 reshape.42.ids_ref
  2.4 0.0 copy-start
  2.4 1.1 %copy-done = bf16[576,576]{1,0:T(8,128)(2,1)S(1)} copy-done((bf16[576,576]{1,0:T(8,128)(2,1)S(1)}, bf16[576,576]{1,0:T(8,128)(2,1)}, u32[]{:S(2)}) %copy-start) | copy-done | bytes 663576
  3.5 0.0 copy-start.1
  3.5 1.1 %copy-done.1 = bf16[576,576]{1,0:T(8,128)(2,1)S(1)} copy-done((bf16[576,576]{1,0:T(8,128)(2,1)S(1)}, bf16[576,576]{1,0:T(8,128)(2,1)}, u32[]{:S(2)}) %copy-start.1) | copy-done | bytes 663576
  4.7 0.0 copy-start.2
  4.7 1.0 %copy-done.2 = bf16[8,6,12,192]{3,0,2,1:T(8,128)(2,1)S(1)} copy-done((bf16[8,6,12,192]{3,0,2,1:T(8,128)(2,1)S(1)}, bf16[8,6,12,192]{3,0,2,1:T(8,128)(2,1)}, u32[]{:S(2)}) %copy-start.2) | copy-done | bytes 221208
  5.6 0.0 copy-start.3
  5.6 1.0 %copy-done.3 = bf16[8,6,12,192]{3,0,2,1:T(8,128)(2,1)S(1)} copy-done((bf16[8,6,12,192]{3,0,2,1:T(8,128)(2,1)S(1)}, bf16[8,6,12,192]{3,0,2,1:T(8,128)(2,1)}, u32[]{:S(2)}) %copy-start.3) | copy-done | bytes 221208
  6.6 0.0 copy-start.4
  6.6 1.0 %copy-done.4 = bf16[384,384]{1,0:T(8,128)(2,1)S(1)} copy-done((bf16[384,384]{1,0:T(8,128)(2,1)S(1)}, bf16[384,384]{1,0:T(8,128)(2,1)}, u32[]{:S(2)}) %copy-start.4) | copy-done | bytes 294936
  7.5 0.0 copy-start.5
  7.5 1.0 %copy-done.5 = bf16[384,384]{1,0:T(8,128)(2,1)S(1)} copy-done((bf16[384,384]{1,0:T(8,128)(2,1)S(1)}, bf16[384,384]{1,0:T(8,128)(2,1)}, u32[]{:S(2)}) %copy-start.5) | copy-done | bytes 294936
  8.5 0.0 copy-start.6
  8.5 0.9 %copy-done.6 = bf16[192,576]{1,0:T(8,128)(2,1)S(1)} copy-done((bf16[192,576]{1,0:T(8,128)(2,1)S(1)}, bf16[192,576]{1,0:T(8,128)(2,1)}, u32[]{:S(2)}) %copy-start.6) | copy-done | bytes 221208
  9.4 0.0 copy-start.7
  9.4 0.9 %copy-done.7 = bf16[192,192]{1,0:T(8,128)(2,1)S(1)} copy-done((bf16[192,192]{1,0:T(8,128)(2,1)S(1)}, bf16[192,192]{1,0:T(8,128)(2,1)}, u32[]{:S(2)}) %copy-start.7) | copy-done | bytes 73752
  10.3 52.6 %shard_map.138 = (bf16[6,2,48,192]{3,2,1,0:T(8,128)(2,1)S(1)}, f32[192,576]{1,0:T(8,128)S(1)}, f32[192,192]{1,0:T(8,128)S(1)}, f32[3456,23]{1,0:T(8,128)S(1)}) custom-call(bf16[6,2,48,192]{3,2,1,0:T(8,128)(2,1)S(1)} %bitcast.22, bf16[6,2,48,192]{3,2,1,0:T(8,128)(2,1)S(1)} %bitcast.23, bf16[192,576]{1,0:T(8,128)(2,1)S(1)} %copy-done.6, ...), custom_call_target="tpu_custom_call" | custom-call | tf_op jit(solution)/shard_map/pallas_call | solution.py:519
  62.9 0.7 %copy.25 = bf16[8,6,12,192]{3,0,2,1:T(8,128)(2,1)} copy(bf16[8,6,12,192]{3,0,2,1:T(8,128)(2,1)S(1)} %bitcast.24) | data formatting | bytes 442368
  63.6 0.8 %copy.26 = f32[192,576]{1,0:T(8,128)} copy(f32[192,576]{1,0:T(8,128)S(1)} %get-tuple-element.17) | data formatting | bytes 884736
  64.4 0.7 %copy.27 = f32[192,192]{1,0:T(8,128)} copy(f32[192,192]{1,0:T(8,128)S(1)} %get-tuple-element.18) | data formatting | bytes 294912
  65.1 1.2 %copy.28 = f32[4,1,6,2,2,6,6,23]{7,4,6,5,3,2,1,0:T(2,128)} copy(f32[4,1,6,2,2,6,6,23]{7,4,6,5,3,2,1,0:T(2,128)S(1)} %bitcast.21) | data formatting | bytes 635904
  (1 shorter events, 0.0 us)
Async XLA Ops:
  2.4 1.1 %copy-start = (bf16[576,576]{1,0:T(8,128)(2,1)S(1)}, bf16[576,576]{1,0:T(8,128)(2,1)}, u32[]{:S(2)}) copy-start(bf16[576,576]{1,0:T(8,128)(2,1)} %constant.21.clone.pt_ref) | copy-start | bytes 1990660
  3.5 1.1 %copy-start.1 = (bf16[576,576]{1,0:T(8,128)(2,1)S(1)}, bf16[576,576]{1,0:T(8,128)(2,1)}, u32[]{:S(2)}) copy-start(bf16[576,576]{1,0:T(8,128)(2,1)} %constant.20.clone.pm_ref) | copy-start | bytes 1990660
  4.7 1.0 %copy-start.2 = (bf16[8,6,12,192]{3,0,2,1:T(8,128)(2,1)S(1)}, bf16[8,6,12,192]{3,0,2,1:T(8,128)(2,1)}, u32[]{:S(2)}) copy-start(bf16[8,6,12,192]{3,0,2,1:T(8,128)(2,1)} %param.11) | copy-start | bytes 663556
  5.6 1.0 %copy-start.3 = (bf16[8,6,12,192]{3,0,2,1:T(8,128)(2,1)S(1)}, bf16[8,6,12,192]{3,0,2,1:T(8,128)(2,1)}, u32[]{:S(2)}) copy-start(bf16[8,6,12,192]{3,0,2,1:T(8,128)(2,1)} %param.12) | copy-start | bytes 663556
  6.6 1.0 %copy-start.4 = (bf16[384,384]{1,0:T(8,128)(2,1)S(1)}, bf16[384,384]{1,0:T(8,128)(2,1)}, u32[]{:S(2)}) copy-start(bf16[384,384]{1,0:T(8,128)(2,1)} %constant.23.clone.gmt_ref) | copy-start | bytes 884740
  7.5 1.0 %copy-start.5 = (bf16[384,384]{1,0:T(8,128)(2,1)S(1)}, bf16[384,384]{1,0:T(8,128)(2,1)}, u32[]{:S(2)}) copy-start(bf16[384,384]{1,0:T(8,128)(2,1)} %constant.22.clone.gm_ref) | copy-start | bytes 884740
  8.5 0.9 %copy-start.6 = (bf16[192,576]{1,0:T(8,128)(2,1)S(1)}, bf16[192,576]{1,0:T(8,128)(2,1)}, u32[]{:S(2)}) copy-start(bf16[192,576]{1,0:T(8,128)(2,1)} %wq_ref.1) | copy-start | bytes 663556
  9.4 0.9 %copy-start.7 = (bf16[192,192]{1,0:T(8,128)(2,1)S(1)}, bf16[192,192]{1,0:T(8,128)(2,1)}, u32[]{:S(2)}) copy-start(bf16[192,192]{1,0:T(8,128)(2,1)} %wp_ref.1) | copy-start | bytes 221188

commit v3 on v2

--- a/solution.py
+++ b/solution.py
@@ -236,9 +236,9 @@
 
 
 def kernel(
-    factor, x_ref, g_ref, wq_ref, wp_ref, tab_ref, ids_ref,
-    pm_ref, pt_ref, gm_ref, gmt_ref,
-    out_x, out_w, out_p, out_b,
+    x_hbm, g_hbm, tab_hbm, gm_hbm, pm_hbm, wq_hbm, wp_hbm, gmt_hbm, pt_hbm, ids_ref,
+    out_x, out_w, out_b,
+    x_ref, g_ref, tab_ref, gm_ref, pm_ref, wq_ref, wp_ref, gmt_ref, pt_ref, fetch_sem,
     pk, sg, hs, og, bias, tabx, tp, fold, dsr, xa, ga, aa, gr, qa, ca, dw,
     ws, wr1, w2, wr2, wl, wm, wf, wo, bs, br, bg, bo,
     halo_send, halo_recv, back_send, back_recv, bsum_send, bsum_recv, ball_send, ball_recv,
@@ -258,6 +258,18 @@
             device_id=where, device_id_type=pl.DeviceIdType.MESH,
         )
 
+    fetches = [
+        pltpu.make_async_copy(src, dst, fetch_sem.at[n])
+        for n, (src, dst) in enumerate(
+            (
+                (x_hbm, x_ref), (g_hbm, g_ref), (tab_hbm, tab_ref), (gm_hbm, gm_ref),
+                (pm_hbm, pm_ref), (wq_hbm, wq_ref), (wp_hbm, wp_ref), (gmt_hbm, gmt_ref),
+                (pt_hbm, pt_ref),
+            )
+        )
+    ]
+    for fetch in fetches:
+        fetch.start()
     barrier = pltpu.get_barrier_semaphore()
     friends = [(1, 0), (2, 0), (3, 0), (0, 1), (0, 2), (0, 3), (1, 1), (-1, -1)]
     for dlon, dlat in friends:
@@ -265,6 +277,8 @@
             barrier, inc=1, device_id=at(dlon, dlat), device_id_type=pl.DeviceIdType.MESH
         )
 
+    fetches[0].wait()
+    fetches[1].wait()
     pk[:, :, :, 0:C] = x_ref[...]
     pk[:, :, :, C : 2 * C] = g_ref[...]
     sg[0:3, 0] = pk[3:6, 1]
@@ -278,6 +292,8 @@
         copy.start()
 
     tabx[...] = jnp.zeros_like(tabx)
+    for fetch in fetches[2:]:
+        fetch.wait()
     for p in range(12):
         tabx[:, 32 * p : 32 * p + 23] = tab_ref[pl.ds(p, 288, stride=12), :]
     table = tabx[...]
@@ -336,22 +352,26 @@
         keyed = jnp.where(usable & (region == lane), 1.0, 0.0).astype(bf16)
         allowed = (dot_nt(hot, keyed) > 0.5) | same
         fold[...] = jnp.zeros_like(fold)
+        held = []
         for h in range(HEADS):
             lo = HEAD_DIM * h
             q = qa[w, :, lo : lo + 32]
             k = qa[w, :, C + lo : C + lo + 32]
             v = qa[w, :, 2 * C + lo : 2 * C + lo + 32]
             go = ca[w, :, lo : lo + 32]
-            scores = dot_nt(q, k) * temper + bias[w, h]
-            scores = jnp.where(allowed, scores, masked_score)
+            held.append((q, k, v, go, dot_nt(q, k), dot_nt(go, v)))
+        ready = []
+        for h, (q, k, v, go, raw, gp) in enumerate(held):
+            scores = jnp.where(allowed, raw * temper + bias[w, h], masked_score)
             power = jnp.exp(scores - jnp.max(scores, axis=-1, keepdims=True))
             probs = power * (1.0 / jnp.sum(power, axis=-1, keepdims=True))
-            low = probs.astype(bf16)
-            aa[w, :, lo : lo + 32] = dot_nn(low, v).astype(bf16)
-            gp = dot_nt(go, v)
             gs = probs * (gp - jnp.sum(probs * gp, axis=-1, keepdims=True))
             dsr[h] = gs
-            scaled = (gs * temper).astype(bf16)
+            ready.append((probs.astype(bf16), (gs * temper).astype(bf16)))
+        for h, (low, scaled) in enumerate(ready):
+            q, k, v, go = held[h][:4]
+            lo = HEAD_DIM * h
+            aa[w, :, lo : lo + 32] = dot_nn(low, v).astype(bf16)
             gr[w, :, lo : lo + 32] = dot_nn(scaled, k).astype(bf16)
             gr[w, :, C + lo : C + lo + 32] = dot_tn(scaled, q).astype(bf16)
             gr[w, :, 2 * C + lo : 2 * C + lo + 32] = dot_tn(low, go).astype(bf16)
@@ -391,6 +411,8 @@
         remote(hs.at[pl.ds(3, 3), 0], og.at[pl.ds(0, 3), 1], back_send.at[1], back_recv.at[1], at(0, 1)),
     ]
 
+    for copy in home:
+        copy.start()
     for s in range(3):
         bias_copy(s).wait()
     total = bs[lon].astype(f32)
@@ -411,8 +433,6 @@
         )
     for copy in wb:
         copy.start()
-    for copy in home:
-        copy.start()
     ball = [
         remote(bg, bo.at[lon], ball_send.at[d - 1], ball_recv.at[d - 1], at(d, 0))
         for d in range(1, 4)
@@ -454,16 +474,30 @@
 
     for copy in ball:
         copy.wait()
+    out_b[...] = bo[...]
+    fourth.wait()
+    out_w[...] = wo[...]
+
+
+def finish(factor, og_hbm, wo_hbm, bo_hbm, out_x, out_w, out_p, out_b, wo, bo, sems):
+    f32 = jnp.float32
+    fetches = [
+        pltpu.make_async_copy(src, dst, sems.at[n])
+        for n, (src, dst) in enumerate(((bo_hbm, bo), (wo_hbm, wo), (og_hbm, out_x)))
+    ]
+    for fetch in fetches:
+        fetch.start()
+    fetches[0].wait()
     for i in range(4):
         piece = bo[i].astype(f32)
         for p in range(12):
             out_b[pl.ds(864 * i + p, 72, stride=12), :] = piece[0:72, 32 * p : 32 * p + 23]
-
-    fourth.wait()
+    fetches[1].wait()
     for n in range(16):
         piece = wo[(n // 4) % 2, n // 8, n % 4].astype(f32) * factor
         out_w[12 * n : 12 * n + 12, :] = piece[0:12, :576]
         out_p[12 * n : 12 * n + 12, :] = piece[0:12, 576:]
+    fetches[2].wait()
 
 
 def fused_body(attn_input, out_grad, w_qkv, w_proj, bias_table, mask_ids, valid_rows):
@@ -486,6 +520,16 @@
     sem = pltpu.SemaphoreType.DMA((3,))
     four = pltpu.SemaphoreType.DMA((4,))
     scratch = [
+        vm((6, 2, PAD, C), bf16),
+        vm((6, 2, PAD, C), bf16),
+        vm((3456, 23), f32),
+        vm((384, 384), bf16),
+        vm((576, 576), bf16),
+        vm((C, 3 * C), bf16),
+        vm((C, C), bf16),
+        vm((384, 384), bf16),
+        vm((576, 576), bf16),
+        pltpu.SemaphoreType.DMA((9,)),
         vm((6, 2, PAD, 2 * C), bf16),
         vm((6, 2, PAD, 2 * C), bf16),
         vm((6, 2, PAD, C), bf16),
@@ -516,21 +560,42 @@
         vm((4, 80, 384), bf16),
     ] + [sem] * 12 + [four] * 2
     whole = pl.BlockSpec(memory_space=pltpu.VMEM)
+    stored = pl.BlockSpec(memory_space=pl.ANY)
+    order_map, order_back, spread_map, spread_back = maps
+    gathered = pl.pallas_call(
+        kernel,
+        out_shape=(
+            jax.ShapeDtypeStruct((6, 2, PAD, C), bf16),
+            jax.ShapeDtypeStruct((2, 2, 4, 16, 768), bf16),
+            jax.ShapeDtypeStruct((4, 80, 384), bf16),
+        ),
+        in_specs=[stored] * 9 + [whole],
+        out_specs=[whole] * 3,
+        scratch_shapes=scratch,
+        compiler_params=pltpu.CompilerParams(
+            collective_id=0, has_side_effects=True, vmem_limit_bytes=VMEM_BYTES
+        ),
+    )(
+        turned(attn_input), turned(out_grad), table, spread_map, order_map,
+        w_qkv, w_proj, spread_back, order_back, codes,
+    )
     grad_input, grad_qkv, grad_proj, folded = pl.pallas_call(
-        functools.partial(kernel, cells ** (-0.5)),
+        functools.partial(finish, cells ** (-0.5)),
         out_shape=(
             jax.ShapeDtypeStruct((6, 2, PAD, C), bf16),
             jax.ShapeDtypeStruct((C, 3 * C), f32),
             jax.ShapeDtypeStruct((C, C), f32),
             jax.ShapeDtypeStruct((3456, 23), f32),
         ),
-        in_specs=[whole] * 10,
+        in_specs=[stored] * 3,
         out_specs=[whole] * 4,
-        scratch_shapes=scratch,
-        compiler_params=pltpu.CompilerParams(
-            collective_id=0, has_side_effects=True, vmem_limit_bytes=48 * 1024 * 1024
-        ),
-    )(turned(attn_input), turned(out_grad), w_qkv, w_proj, table, codes, *maps)
+        scratch_shapes=[
+            vm((2, 2, 4, 16, 768), bf16),
+            vm((4, 80, 384), bf16),
+            pltpu.SemaphoreType.DMA((3,)),
+        ],
+        compiler_params=pltpu.CompilerParams(vmem_limit_bytes=VMEM_BYTES),
+    )(*gathered)
     grad_input = grad_input.reshape(6, 12, 8, C).transpose(2, 0, 1, 3)
     folded = folded.reshape(4, 1, 6, 2, 6, 6, 2, 23)
     return grad_input, grad_qkv, grad_proj, folded.transpose(0, 1, 2, 3, 6, 4, 5, 7)
@@ -546,6 +611,7 @@
 
 
 PAD = 48
+VMEM_BYTES = 60 * 1024 * 1024
 
 
 def solution(mesh):

time: 66.8 us -> 53.7 us (0.80)
  local copies, waits for them, and re-layouts: 11.6 us -> 1.02 us
  Pallas kernels: 52.6 us -> 50.3 us
    unnamed x20 -> x0, local copies, waits for them, and re-layouts: 11.3 us -> none
    pallas_call x1 -> x2, Pallas kernels: 52.6 us -> 50.3 us  [the longest x1 47.4 us: fused_body(): pl.pallas_call(kernel, out_shape=(jax.ShapeDtypeStruct((6, 2, PAD, C), bf...]
    reshape x2, local copies, waits for them, and re-layouts: 0.3 us -> 1.02 us  [fused_body(): codes = codes.reshape(4, 2, 6, 12).transpose(0, 3, 1, 2).reshape(4, WIN, 1)]
where the time goes in v3:
time: 53.7 us; the launch traced here: 53.4 us
  Pallas kernels  50.3 us (94%)
  between operations  1.3 us (2%)
  local copies, waits for them, and re-layouts  1.02 us (2%)
  other arithmetic  0.82 us (2%)
    pallas_call x1, Pallas kernels, fused_body(): pl.pallas_call(kernel, out_shape=(jax.ShapeDtypeStruct((6, 2, PAD, C), bf...  47.4 us
    pallas_call x1, Pallas kernels, fused_body(): pl.pallas_call(functools.partial(finish, cells ** (-0.5)), out_shape=(jax...  2.95 us

profile of v3, /device:TPU:0, one launch (start us, length us, event | category | flops | bytes accessed | tf_op | source)
XLA Modules:
  0.0 53.4 jit_solution(15003569109881419637)
XLA Ops:
  1.3 0.8 %add_select_fusion = s32[8,6,12]{2,0,1:T(8,128)S(1)} fusion(s32[8,6,12]{2,0,1:T(8,128)} %param.16, pred[6]{0:T(512)(128)(4,1)S(1)} %add_compare_fusion), kind=kLoop, calls=%fused_computation | loop fusion | flops 1152 | bytes 4614 | tf_op jit(solution)/shard_map/jit(_where)/select_n | solution.py:508
  2.1 0.1 copy.17
  2.2 0.9 %reshape.42.ids_ref = s32[4,144,1]{2,1,0:T(8,128)} reshape(s32[4,12,2,6]{3,2,1,0:T(2,128)S(1)} %bitcast.24) | data formatting | bytes 4608 | tf_op jit(solution)/shard_map/reshape | solution.py:509
  3.1 47.4 %shard_map.138 = (bf16[6,2,48,192]{3,2,1,0:T(8,128)(2,1)}, bf16[2,2,4,16,768]{4,3,2,1,0:T(8,128)(2,1)}, bf16[4,80,384]{2,1,0:T(8,128)(2,1)}) custom-call(bf16[6,2,48,192]{3,2,1,0:T(8,128)(2,1)} %bitcast.22, bf16[6,2,48,192]{3,2,1,0:T(8,128)(2,1)} %bitcast.23, f32[3456,23]{1,0:T(8,128)} %bitcast.21, bf16[384,384]{1,0:T(8,128)(2,1)} %constant.22.clone.gm_hbm, ...), custom_call_target="tpu_custom_call" | custom-call | tf_op jit(solution)/shard_map/pallas_call | solution.py:565
  50.5 3.0 %shard_map.139 = (bf16[6,2,48,192]{3,2,1,0:T(8,128)(2,1)}, f32[192,576]{1,0:T(8,128)}, f32[192,192]{1,0:T(8,128)}, f32[3456,23]{1,0:T(8,128)}) custom-call(bf16[6,2,48,192]{3,2,1,0:T(8,128)(2,1)} %get-tuple-element.11.og_hbm, bf16[2,2,4,16,768]{4,3,2,1,0:T(8,128)(2,1)} %get-tuple-element.12.wo_hbm, bf16[4,80,384]{2,1,0:T(8,128)(2,1)} %get-tuple-element.13.bo_hbm), custom_call_target="tpu_custom_call" | custom-call | tf_op jit(solution)/shard_map/pallas_call | solution.py:582
  (1 shorter events, 0.0 us)

commit v4 on v3

--- a/solution.py
+++ b/solution.py
@@ -386,7 +386,7 @@
 
         return carry
 
-    lax.fori_loop(0, 4, window, 0)
+    lax.fori_loop(0, 4, window, 0, unroll=True)
 
     grads = gr[...].reshape(576, 576)
     dw[:, :576] = dot_tn(xa[...], grads)

time: 53.7 us -> 52.1 us (0.970)
  Pallas kernels: 50.3 us -> 48.8 us
    pallas_call x1, Pallas kernels: 47.4 us -> 45.8 us  [fused_body(): pl.pallas_call(kernel, out_shape=(jax.ShapeDtypeStruct((6, 2, PAD, C), bf...]
where the time goes in v4:
time: 52.1 us; the launch traced here: 51.9 us
  Pallas kernels  48.8 us (94%)
  between operations  1.3 us (2%)
  local copies, waits for them, and re-layouts  1.02 us (2%)
  other arithmetic  0.82 us (2%)
    pallas_call x1, Pallas kernels, fused_body(): pl.pallas_call(kernel, out_shape=(jax.ShapeDtypeStruct((6, 2, PAD, C), bf...  45.8 us
    pallas_call x1, Pallas kernels, fused_body(): pl.pallas_call(functools.partial(finish, cells ** (-0.5)), out_shape=(jax...  2.95 us

profile of v4, /device:TPU:0, one launch (start us, length us, event | category | flops | bytes accessed | tf_op | source)
XLA Modules:
  0.0 51.9 jit_solution(9413689642468965835)
XLA Ops:
  1.3 0.8 %add_select_fusion = s32[8,6,12]{2,0,1:T(8,128)S(1)} fusion(s32[8,6,12]{2,0,1:T(8,128)} %param.16, pred[6]{0:T(512)(128)(4,1)S(1)} %add_compare_fusion), kind=kLoop, calls=%fused_computation | loop fusion | flops 1152 | bytes 4614 | tf_op jit(solution)/shard_map/jit(_where)/select_n | solution.py:508
  2.1 0.1 copy.17
  2.2 0.9 %reshape.42.ids_ref = s32[4,144,1]{2,1,0:T(8,128)} reshape(s32[4,12,2,6]{3,2,1,0:T(2,128)S(1)} %bitcast.24) | data formatting | bytes 4608 | tf_op jit(solution)/shard_map/reshape | solution.py:509
  3.1 45.8 %shard_map.138 = (bf16[6,2,48,192]{3,2,1,0:T(8,128)(2,1)}, bf16[2,2,4,16,768]{4,3,2,1,0:T(8,128)(2,1)}, bf16[4,80,384]{2,1,0:T(8,128)(2,1)}) custom-call(bf16[6,2,48,192]{3,2,1,0:T(8,128)(2,1)} %bitcast.22, bf16[6,2,48,192]{3,2,1,0:T(8,128)(2,1)} %bitcast.23, f32[3456,23]{1,0:T(8,128)} %bitcast.21, bf16[384,384]{1,0:T(8,128)(2,1)} %constant.22.clone.gm_hbm, ...), custom_call_target="tpu_custom_call" | custom-call | tf_op jit(solution)/shard_map/pallas_call | solution.py:565
  49.0 3.0 %shard_map.139 = (bf16[6,2,48,192]{3,2,1,0:T(8,128)(2,1)}, f32[192,576]{1,0:T(8,128)}, f32[192,192]{1,0:T(8,128)}, f32[3456,23]{1,0:T(8,128)}) custom-call(bf16[6,2,48,192]{3,2,1,0:T(8,128)(2,1)} %get-tuple-element.11.og_hbm, bf16[2,2,4,16,768]{4,3,2,1,0:T(8,128)(2,1)} %get-tuple-element.12.wo_hbm, bf16[4,80,384]{2,1,0:T(8,128)(2,1)} %get-tuple-element.13.bo_hbm), custom_call_target="tpu_custom_call" | custom-call | tf_op jit(solution)/shard_map/pallas_call | solution.py:582
  (1 shorter events, 0.0 us)
